TPU v7x, 768 devices: a whole 4x8x12 slice. The times are simulated.
768 devices in a mesh: group: 96 (over z, y), local: 8 (over x, core).
Axes of the slice: x: 4, y: 8, z: 12, core: 2. Of those that a mesh axis runs over, the one named last changes fastest.
Arguments:
- features: bfloat16 [786432, 256], P(('group', 'local')), may hold values from -6 to 6
- aggregate: bfloat16 [786432, 256], P(('group', 'local')), may hold values from -6 to 6
- preact: bfloat16 [786432, 256], P(('group', 'local')), may hold values from -8 to 8
- cotangent: bfloat16 [786432, 256], P(('group', 'local')), may hold values from -6 to 6
- w_self: bfloat16 [256, 256], replicated, may hold values from -0.375 to 0.375
- w_neigh: bfloat16 [256, 256], replicated, may hold values from -0.375 to 0.375
- tile_vals: bfloat16 [49152, 128, 128], P(('group', 'local')), may hold values from -0.1875 to 0.1875
- tile_rows: int32 [49152], P(('group', 'local')), may hold values from 0 to 7
- tile_cols: int32 [49152], P(('group', 'local')), may hold values from 0 to 7
- edge_dst: int32 [1572864], P(('group', 'local')), may hold values from 0 to 1023
- edge_slot: int32 [1572864], P(('group', 'local')), may hold values from 0 to 1535
- edge_weight: float32 [1572864], P(('group', 'local')), may hold values from 0.1 to 1
- recv_rows: int32 [96, 96, 16], P('group', None, 'local'), may hold values from 0 to 1023
Outputs:
- grad_x: bfloat16 [786432, 256], P(('group', 'local'))
- grad_self_w: float32 [256, 256], replicated
- grad_neigh_w: float32 [256, 256], replicated
All inputs are finite; a program needn't handle non-finite values.
Results may differ from a plain program's by a relative error of at most 0.014.
Values may be sent and summed in bfloat16 or wider, within the bound.
No kernel may reach another device: no remote copies, remote signals or barrier semaphores. Data moves between devices by JAX's collectives and lax.ppermute only.
A program may use at most 64 MiB of HBM per device.

v0:
```python
import jax
import jax.numpy as jnp
from jax import lax
from jax.sharding import PartitionSpec as P


def rows_product(first_op, second_op):
    return lax.dot_general(
        first_op, second_op, (((0,), (0,)), ((), ())), preferred_element_type=jnp.float32
    )


def times_transposed(first_op, second_op):
    return lax.dot_general(
        first_op, second_op, (((1,), (1,)), ((), ())), preferred_element_type=jnp.float32
    )


def on_device(
    features,
    aggregate,
    preact,
    cotangent,
    w_self,
    w_neigh,
    tile_vals,
    tile_rows,
    tile_cols,
    edge_dst,
    edge_slot,
    edge_weight,
    recv_rows,
):
    groups = lax.axis_size("group")
    members = lax.axis_size("local")
    node_count = features.shape[0]
    feat_width = features.shape[1]
    block_size = tile_vals.shape[1]
    blocks = node_count // block_size
    per_owner = recv_rows.shape[2]
    grad_scale = (node_count * groups * members) ** (-0.5)
    preact_f = preact.astype(jnp.float32)
    gate_sig = jax.nn.sigmoid(preact_f)
    d_preact = (
        cotangent.astype(jnp.float32) * gate_sig * (1.0 + preact_f * (1.0 - gate_sig))
    ).astype(jnp.bfloat16)
    pushed = times_transposed(d_preact, w_neigh).astype(jnp.bfloat16)
    edge_terms = jnp.take(pushed, edge_dst, axis=0).astype(jnp.float32) * edge_weight[:, None]
    partial_value = jax.ops.segment_sum(
        edge_terms, edge_slot, num_segments=groups * members * per_owner
    )
    partial_value = partial_value.reshape(groups, members, per_owner, feat_width)
    summed = lax.psum_scatter(
        partial_value.astype(jnp.bfloat16), "local", scatter_dimension=1, tiled=True
    )
    arrived = lax.all_to_all(summed, "group", split_axis=0, concat_axis=0, tiled=True)
    weight_grads = (
        jnp.stack([rows_product(features, d_preact), rows_product(aggregate, d_preact)])
        * grad_scale
    )
    weight_grads = lax.psum(weight_grads, ("group", "local"))
    own_term = times_transposed(d_preact, w_self)
    src_blocks = jnp.take(pushed.reshape(blocks, block_size, feat_width), tile_rows, axis=0)
    contrib = jnp.einsum("tij,tih->tjh", tile_vals, src_blocks, preferred_element_type=jnp.float32)
    interior = jax.ops.segment_sum(contrib, tile_cols, num_segments=blocks).reshape(
        node_count, feat_width
    )
    incoming = jax.ops.segment_sum(
        arrived.reshape(groups * per_owner, feat_width).astype(jnp.float32),
        recv_rows.reshape(groups * per_owner),
        num_segments=node_count,
    )
    grad_x = (own_term + interior + incoming).astype(jnp.bfloat16)
    return (grad_x, weight_grads[0], weight_grads[1])


def solution(mesh):
    placed = (
        P(("group", "local"), None),
        P(("group", "local"), None),
        P(("group", "local"), None),
        P(("group", "local"), None),
        P(),
        P(),
        P(("group", "local"), None, None),
        P(("group", "local")),
        P(("group", "local")),
        P(("group", "local")),
        P(("group", "local")),
        P(("group", "local")),
        P("group", None, "local"),
    )
    return jax.shard_map(
        on_device,
        mesh=mesh,
        in_specs=placed,
        out_specs=(P(("group", "local"), None), P(), P()),
        check_vma=False,
    )
```

profile of v0, /device:TPU:1, one launch (start us, length us, event | category | flops | bytes accessed | tf_op | source)
XLA Modules:
  0.0 528.6 jit_solution(4924712076958663448)
XLA Ops:
  8.0 0.0 copy-start
  8.0 0.0 copy-start.4
  8.0 0.0 reduce-scatter.2.cloned.1.call-start
  8.1 0.8 fusion.21
  8.9 0.7 compare_and_fusion
  9.6 1.6 fusion.15
  11.3 0.0 copy-start.1
  11.3 1.4 convolution_convert_fusion
  12.6 0.0 copy-done.4
  12.7 19.7 %scatter_custom_fusion.1 = f32[1536,256]{1,0:T(8,128)} fusion(s32[2048]{0:T(1024)} %param.23, f32[2048]{0:T(1024)S(1)} %copy-done.4, pred[2048]{0:T(1024)(128)(4,1)S(1)} %compare_and_fusion, f32[]{:T(128)} %constant.19.clone.1, bf16[]{:T(256)} %constant.34.clone.1, bf16[1024,256]{1,0:T(8,128)(2,1)S(1)} %convolution_convert_fusion, s32[2048]{0:T(1024)S(1)} %fusion.21), kind=kCustom, calls=%fused_computation.9 | custom fusion | flops 2097152 | bytes 2116608 | tf_op jit(solution)/shard_map/scatter-add | solution.py:49
  32.4 2.4 convert_element_type.35
  34.7 2.8 convert_element_type.36
  37.6 2.3 copy.34
  39.8 0.0 reduce-scatter.2.cloned.1.call-update
  39.9 0.0 copy-start.7
  39.9 0.0 all-reduce.2.cloned.1.call-start
  39.9 1.4 convolution_bitcast_fusion
  41.3 0.0 copy-done.1
  41.3 1.4 convolution_bitcast_fusion.1
  42.7 0.9 maximum_multiply_fusion
  43.6 0.0 all-reduce.2.cloned.1.call-update
  43.6 0.0 copy-done.7
  43.7 2.8 gather_fusion
  46.4 0.0 copy-done
  46.4 6.8 %fusion.3 = f32[64,128,256]{1,2,0:T(8,128)} fusion(bf16[64,128,128]{2,1,0:T(8,128)(2,1)S(1)} %copy-done, bf16[64,128,256]{2,1,0:T(8,128)(2,1)} %gather_fusion, pred[64]{0:T(512)(128)(4,1)S(1)} %compare_and_fusion.1), kind=kOutput, calls=%fused_computation.8 | convolution fusion | flops 538968064 | bytes 14680128 | tf_op jit(solution)/shard_map/tij,tih->tjh/dot_general | solution.py:64
  53.2 0.0 copy-start.6
  53.2 9.0 %copy.32 = f32[64,128,256]{2,1,0:T(8,128)} copy(f32[64,128,256]{1,2,0:T(8,128)} %fusion.3) | data formatting | bytes 16777216 | tf_op jit(solution)/shard_map/tij,tih->tjh/dot_general | solution.py:64
  62.2 0.1 broadcast_in_dim.38
  62.3 0.0 copy-done.6
  62.3 0.0 copy-start.3
  62.3 12.4 %scatter_fusion = f32[8,128,256]{2,1,0:T(8,128)S(1)} fusion(f32[8,128,256]{2,1,0:T(8,128)S(1)} %broadcast_in_dim.38, s32[64]{0:T(128)S(1)} %copy-done.6, f32[64,128,256]{2,1,0:T(8,128)} %copy.32), kind=kCustom, calls=%fused_computation.2 | custom fusion | flops 2097152 | bytes 25166080 | tf_op jit(solution)/shard_map/scatter-add | solution.py:65
  74.7 0.0 copy-start.5
  74.7 11.4 %reduce-scatter.2.cloned.1.call-done = bf16[96,1,2,256]{3,0,2,1:T(8,128)(2,1)} async-done(((bf16[96,8,2,256]{3,0,2,1:T(8,128)(2,1)}), bf16[96,1,2,256]{3,0,2,1:T(8,128)(2,1)}) %reduce-scatter.2.cloned.1.call-update) | async-done | bytes 98320 | tf_op jit(solution)/shard_map/reduce_scatter | solution.py:53
  86.1 1.6 copy.35
  87.8 14.9 %all-to-all-start = ((bf16[96,1,2,256]{3,2,1,0:T(2,128)(2,1)}), bf16[96,1,2,256]{3,2,1,0:T(2,128)(2,1)S(1)}, u32[]{:S(2)}, u32[]{:S(2)}) async-start(bf16[96,1,2,256]{3,2,1,0:T(2,128)(2,1)} %copy.35), calls=%async_computation.1 | async-start | bytes 196608 | tf_op jit(solution)/shard_map/all_to_all | solution.py:56
  102.7 0.0 copy-done.3
  102.7 2.4 convolution_add_fusion
  105.1 0.0 copy-done.5
  105.1 0.0 copy-start.2
  105.1 0.1 copy.33
  105.2 0.1 reshape.65
  105.3 408.6 %all-reduce.2.cloned.1.call-done = f32[2,256,256]{1,2,0:T(8,128)} async-done(((f32[2,256,256]{1,2,0:T(8,128)}), f32[2,256,256]{1,2,0:T(8,128)}) %all-reduce.2.cloned.1.call-update) | async-done | bytes 524304 | tf_op jit(solution)/shard_map/psum | solution.py:61
  513.9 1.8 slice_bitcast_fusion
  515.7 1.8 copy.36
  517.4 0.8 copy.37
  518.3 0.0 all-to-all-done
  518.3 0.0 copy-done.2
  518.3 2.0 scatter_fusion.1
  520.4 0.8 convert_element_type.39
  (4 shorter events, 0.0 us)
Async XLA Ops:
  8.0 38.4 %copy-start = (bf16[64,128,128]{2,1,0:T(8,128)(2,1)S(1)}, bf16[64,128,128]{2,1,0:T(8,128)(2,1)}, u32[]{:S(2)}) copy-start(bf16[64,128,128]{2,1,0:T(8,128)(2,1)} %param.19) | copy-start | bytes 6291460
  8.0 4.6 copy-start.4
  8.0 78.1 %reduce-scatter.2.cloned.1.call-start = ((), (), s32[]{:S(2)}) async-start(), calls=%async_computation.2 | async-start | bytes 884736 | tf_op jit(solution)/shard_map/reduce_scatter | solution.py:53
  11.3 30.1 %copy-start.1 = (bf16[1024,256]{1,0:T(8,128)(2,1)}, bf16[1024,256]{1,0:T(8,128)(2,1)S(1)}, u32[]{:S(2)}) copy-start(bf16[1024,256]{1,0:T(8,128)(2,1)S(1)} %fusion.15) | copy-start | bytes 1572868
  39.9 3.7 copy-start.7
  39.9 474.0 %all-reduce.2.cloned.1.call-start = ((), (), s32[]{:S(2)}) async-start(), calls=%async_computation.3 | async-start | bytes 1048576 | tf_op jit(solution)/shard_map/psum | solution.py:61
  53.2 9.1 %copy-start.6 = (s32[64]{0:T(128)S(1)}, s32[64]{0:T(128)}, u32[]{:S(2)}) copy-start(s32[64]{0:T(128)} %param.21) | copy-start | bytes 772
  62.3 40.4 %copy-start.3 = (bf16[256,256]{1,0:T(8,128)(2,1)S(1)}, bf16[256,256]{1,0:T(8,128)(2,1)}, u32[]{:S(2)}) copy-start(bf16[256,256]{1,0:T(8,128)(2,1)} %param.17) | copy-start | bytes 393220
  74.7 30.3 %copy-start.5 = (s32[1,96,2]{1,2,0:T(2,128)S(1)}, s32[1,96,2]{1,2,0:T(2,128)}, u32[]{:S(2)}) copy-start(s32[1,96,2]{1,2,0:T(2,128)} %param.25) | copy-start | bytes 2308
  87.8 430.5 %all-to-all-start = ((bf16[96,1,2,256]{3,2,1,0:T(2,128)(2,1)}), bf16[96,1,2,256]{3,2,1,0:T(2,128)(2,1)S(1)}, u32[]{:S(2)}, u32[]{:S(2)}) async-start(bf16[96,1,2,256]{3,2,1,0:T(2,128)(2,1)} %copy.35), calls=%async_computation.1 | async-start | bytes 196608 | tf_op jit(solution)/shard_map/all_to_all | solution.py:56
  105.1 413.3 %copy-start.2 = (f32[1024,256]{1,0:T(8,128)S(1)}, f32[1024,256]{1,0:T(8,128)}, u32[]{:S(2)}) copy-start(f32[1024,256]{1,0:T(8,128)} %convolution_add_fusion) | copy-start | bytes 3145732
Sparse Core Ops, SparseCore 0:
  40.0 46.1 reduce-scatter.1
Sparse Core Ops, SparseCore 1:
  46.6 467.2 all-reduce.1
where the time goes:
time: 530 us; the launch traced here: 529 us
  waiting for transfers between devices  420 us (79%)
  other arithmetic  41.4 us (8%)
  local copies, waits for them, and re-layouts  23.3 us (4%)
  between operations  15.7 us (3%)
  starting transfers between devices  15 us (3%)
  matrix products  13.3 us (3%)
    psum x1, waiting for transfers between devices, on_device(): weight_grads = lax.psum(weight_grads, ('group', 'local'))  409 us
    scatter-add x1, other arithmetic, on_device(): jax.ops.segment_sum(edge_terms, edge_slot, num_segments=groups * members...  19.7 us
    all_to_all x1, starting transfers between devices, on_device(): lax.all_to_all(summed, 'group', split_axis=0, concat_axis=0, tiled=True)  14.9 us
    scatter-add x1, other arithmetic, on_device(): jax.ops.segment_sum(contrib, tile_cols, num_segments=blocks)  12.4 us
    reduce_scatter x1, waiting for transfers between devices, on_device(): lax.psum_scatter(partial_value.astype(jnp.bfloat16), 'local', scatter_dim...  11.4 us
  transfers between devices with their start and end apart: 3, of which 2 were waited for; matrix products, arithmetic and copies ran while one was open for 8% of the time, Pallas kernels for 0%

commit v1 on v0

v1 whole, which is shorter than its diff:
```python
import jax
import jax.numpy as jnp
from jax import lax
from jax.experimental import pallas as pl
from jax.experimental.pallas import tpu as pltpu
from jax.sharding import PartitionSpec as P

F32 = jnp.float32
BF16 = jnp.bfloat16
VMEM_LIMIT = 48 * 1024 * 1024


def dot_nn(first_op, second_op):
    return lax.dot_general(first_op, second_op, (((1,), (0,)), ((), ())), preferred_element_type=F32)


def dot_nt(first_op, second_op):
    return lax.dot_general(first_op, second_op, (((1,), (1,)), ((), ())), preferred_element_type=F32)


def identity(size):
    row = lax.broadcasted_iota(jnp.int32, (size, size), 0)
    col = lax.broadcasted_iota(jnp.int32, (size, size), 1)
    return jnp.where(row == col, 1.0, 0.0).astype(BF16)


def edges_and_grads(groups, members, per_owner, scale, chunk):
    def kernel(
        preact_ref, cot_ref, feat_ref, agg_ref, wn_ref, dst_ref, slot_ref, weight_ref, dp_ref, pushed_ref, part_ref
    ):
        nodes, width = preact_ref.shape
        edges = dst_ref.shape[1]
        x = preact_ref[...].astype(F32)
        sig = jax.nn.sigmoid(x)
        dp = (cot_ref[...].astype(F32) * sig * (1.0 + x * (1.0 - sig))).astype(BF16)
        dp_ref[...] = dp
        pushed_t = dot_nt(wn_ref[...], dp).astype(BF16)
        pushed_ref[...] = pushed_t

        eye = identity(width)
        rows_per_member = 2 * width // members
        per_grad = width // rows_per_member
        for which, ref in enumerate((feat_ref, agg_ref)):
            ref_t = dot_nt(eye, ref[...]).astype(BF16)
            grad = (dot_nn(ref_t, dp) * scale).astype(BF16)
            for k in range(per_grad):
                m = which * per_grad + k
                part_ref[m, 0:rows_per_member, per_owner * width :] = grad[
                    k * rows_per_member : (k + 1) * rows_per_member
                ]
                part_ref[m, rows_per_member:, per_owner * width :] = jnp.zeros(
                    (groups - rows_per_member, width), BF16
                )

        rows = members * groups
        for e0 in range(0, edges, chunk):
            dst = dst_ref[:, e0 : e0 + chunk]
            node = lax.broadcasted_iota(jnp.int32, (nodes, chunk), 0)
            take = jnp.where(node == dst, 1.0, 0.0).astype(BF16)
            terms = (dot_nn(pushed_t, take) * weight_ref[:, e0 : e0 + chunk]).astype(BF16)
            terms_ref_value = terms
            if e0 == 0:
                all_terms = [terms_ref_value]
            else:
                all_terms.append(terms_ref_value)
        terms = jnp.concatenate(all_terms, axis=1)

        slot = slot_ref[...]
        per_group = members * per_owner
        group = slot // per_group
        rest = slot - group * per_group
        member = rest // per_owner
        which = rest - member * per_owner
        place = which * rows + member * groups + group
        for j in range(per_owner):
            for m in range(members):
                base = j * rows + m * groups
                row = lax.broadcasted_iota(jnp.int32, (groups, edges), 0) + base
                put = jnp.where(row == place, 1.0, 0.0).astype(BF16)
                part_ref[m, :, j * width : (j + 1) * width] = dot_nt(put, terms).astype(BF16)

    return kernel


def tiles_kernel(rows_ref, cols_ref, vals_ref, pushed_ref, dp_ref, ws_ref, out_ref, adj_ref):
    count, block, _ = vals_ref.shape
    adj_ref[...] = jnp.zeros_like(adj_ref)

    def add(t, carry):
        at = (pl.ds(rows_ref[t] * block, block), pl.ds(pl.multiple_of(cols_ref[t] * block, block), block))
        adj_ref[at] += vals_ref[t].astype(F32)
        return carry

    lax.fori_loop(0, count, add, 0)
    interior_t = dot_nn(pushed_ref[...], adj_ref[...].astype(BF16))
    out_ref[...] = dot_nt(dp_ref[...], ws_ref[...]) + interior_t.T


def finish_kernel(arrived_ref, target_ref, base_ref, out_ref, row_ref):
    nodes, width = out_ref.shape
    groups = arrived_ref.shape[0]
    per_owner = target_ref.shape[0]
    arrived = arrived_ref[...]
    total = base_ref[...]
    for j in range(per_owner):
        node = lax.broadcasted_iota(jnp.int32, (nodes, groups), 0)
        put = jnp.where(node == target_ref[j : j + 1, :], 1.0, 0.0).astype(BF16)
        total += dot_nn(put, arrived[:, j * width : (j + 1) * width])
    out_ref[...] = total.astype(BF16)
    row_ref[...] = jnp.sum(
        arrived[:, per_owner * width :].astype(F32), axis=0, keepdims=True
    ).astype(BF16)


def on_device(
    features,
    aggregate,
    preact,
    cotangent,
    w_self,
    w_neigh,
    tile_vals,
    tile_rows,
    tile_cols,
    edge_dst,
    edge_slot,
    edge_weight,
    recv_rows,
):
    groups = lax.axis_size("group")
    members = lax.axis_size("local")
    nodes, width = features.shape
    edges = edge_dst.shape[0]
    per_owner = recv_rows.shape[2]
    scale = (nodes * groups * members) ** (-0.5)
    payload = (per_owner + 1) * width
    share = 2 * width // members
    params = pltpu.CompilerParams(vmem_limit_bytes=VMEM_LIMIT)

    dp, pushed_t, part = pl.pallas_call(
        edges_and_grads(groups, members, per_owner, scale, 512),
        out_shape=(
            jax.ShapeDtypeStruct((nodes, width), BF16),
            jax.ShapeDtypeStruct((width, nodes), BF16),
            jax.ShapeDtypeStruct((members, groups, payload), BF16),
        ),
        compiler_params=params,
        name="edges_and_grads",
    )(
        preact,
        cotangent,
        features,
        aggregate,
        w_neigh,
        edge_dst.reshape(1, edges),
        edge_slot.reshape(1, edges),
        edge_weight.reshape(1, edges),
    )
    smem = pl.BlockSpec(memory_space=pltpu.SMEM)
    vmem = pl.BlockSpec(memory_space=pltpu.VMEM)
    base = pl.pallas_call(
        tiles_kernel,
        out_shape=jax.ShapeDtypeStruct((nodes, width), F32),
        in_specs=[smem, smem, vmem, vmem, vmem, vmem],
        scratch_shapes=[pltpu.VMEM((nodes, nodes), F32)],
        compiler_params=params,
        name="tiles",
    )(tile_rows, tile_cols, tile_vals, pushed_t, dp, w_self)

    part = lax.all_to_all(part, "local", 0, 0, tiled=True)
    summed = part.astype(F32).sum(0).astype(BF16)
    arrived = lax.all_to_all(summed, "group", 0, 0, tiled=True)
    grad_x, row = pl.pallas_call(
        finish_kernel,
        out_shape=(
            jax.ShapeDtypeStruct((nodes, width), BF16),
            jax.ShapeDtypeStruct((1, width), BF16),
        ),
        compiler_params=params,
        name="finish",
    )(arrived, recv_rows.reshape(groups, per_owner).T, base)
    spread = lax.all_to_all(jnp.broadcast_to(row, (groups, width)), "group", 0, 0, tiled=True)
    mine = spread[:share]
    grads = lax.all_to_all(jnp.broadcast_to(mine[None], (members, share, width)), "local", 0, 0, tiled=True)
    grads = grads.reshape(2, width, width).astype(F32)
    return (grad_x, grads[0], grads[1])


def solution(mesh):
    both = ("group", "local")
    placed = (
        P(both, None),
        P(both, None),
        P(both, None),
        P(both, None),
        P(),
        P(),
        P(both, None, None),
        P(both),
        P(both),
        P(both),
        P(both),
        P(both),
        P("group", None, "local"),
    )
    return jax.shard_map(
        on_device,
        mesh=mesh,
        in_specs=placed,
        out_specs=(P(both, None), P(), P()),
        check_vma=False,
    )
```

time: 530 us -> 114 us (0.22)
  waiting for transfers between devices: 420 us -> 9.66 us
  blocking collectives: 0 us -> 60.8 us
  other arithmetic: 41.4 us -> 3.37 us
  between operations: 15.7 us -> 0.79 us
  matrix products: 13.3 us -> 0 us
  Pallas kernels: 0 us -> 10.7 us
  local copies, waits for them, and re-layouts: 23.3 us -> 13.2 us
    psum x1 -> x0, waiting for transfers between devices: 409 us -> none  [on_device(): weight_grads = lax.psum(weight_grads, ('group', 'local'))]
    all_to_all x0 -> x3, blocking collectives: none -> 60.8 us  [the longest x1 29.7 us: on_device(): part = lax.all_to_all(part, 'local', 0, 0, tiled=True)]
    scatter-add x3 -> x0, other arithmetic: 34.1 us -> none  [the longest x1 19.7 us: on_device(): jax.ops.segment_sum(edge_terms, edge_slot, num_segments=groups * members...]
    dot_general x5 -> x0, matrix products: 13.3 us -> none  [the longest x1 6.8 us: on_device(): jnp.einsum('tij,tih->tjh', tile_vals, src_blocks, preferred_element_type=...]
    reduce_scatter x1 -> x0, waiting for transfers between devices: 11.4 us -> none  [on_device(): lax.psum_scatter(partial_value.astype(jnp.bfloat16), 'local', scatter_dim...]
    pallas_call x0 -> x3, Pallas kernels: none -> 10.7 us  [the longest x1 6.8 us: on_device(): pl.pallas_call(edges_and_grads(groups, members, per_owner, scale, 512), o...]
    all_to_all x1, waiting for transfers between devices: 0.01 us -> 9.66 us  [on_device(): arrived = lax.all_to_all(summed, 'group', 0, 0, tiled=True)]
    dot_general x1 -> x0, local copies, waits for them, and re-layouts: 9.01 us -> none  [on_device(): jnp.einsum('tij,tih->tjh', tile_vals, src_blocks, preferred_element_type=...]
  transfers between devices with their start and end apart: 3 -> 1, of which waited for: 2 -> 1; matrix products, arithmetic and copies ran while one was open for 8% -> 0% of each run, Pallas kernels for 0% -> 2%
where the time goes in v1:
time: 114 us; the launch traced here: 113 us
  blocking collectives  60.8 us (53%)
  starting transfers between devices  14.4 us (13%)
  local copies, waits for them, and re-layouts  13.2 us (12%)
  Pallas kernels  10.7 us (9%)
  waiting for transfers between devices  9.66 us (8%)
  other arithmetic  3.37 us (3%)
    all_to_all x1, blocking collectives, on_device(): part = lax.all_to_all(part, 'local', 0, 0, tiled=True)  29.7 us
    all_to_all x1, blocking collectives, on_device(): lax.all_to_all(jnp.broadcast_to(row, (groups, width)), 'group', 0, 0, til...  18.5 us
    all_to_all x1, starting transfers between devices, on_device(): arrived = lax.all_to_all(summed, 'group', 0, 0, tiled=True)  14.4 us
    all_to_all x1, blocking collectives, on_device(): lax.all_to_all(jnp.broadcast_to(mine[None], (members, share, width)), 'lo...  12.7 us
    unnamed x40, local copies, waits for them, and re-layouts  11.7 us
    all_to_all x1, waiting for transfers between devices, on_device(): arrived = lax.all_to_all(summed, 'group', 0, 0, tiled=True)  9.66 us
    pallas_call x1, Pallas kernels, on_device(): pl.pallas_call(edges_and_grads(groups, members, per_owner, scale, 512), o...  6.8 us
    pallas_call x1, Pallas kernels, on_device(): pl.pallas_call(tiles_kernel, out_shape=jax.ShapeDtypeStruct((nodes, width...  2.7 us
  transfers between devices with their start and end apart: 1, of which 1 were waited for; matrix products, arithmetic and copies ran while one was open for 0% of the time, Pallas kernels for 2%

profile of v1, /device:TPU:1, one launch (start us, length us, event | category | flops | bytes accessed | tf_op | source)
XLA Modules:
  0.0 113.0 jit_solution(15151541668671160525)
XLA Ops:
  0.6 0.0 copy-start.1
  0.6 1.0 copy-done.1
  1.7 0.0 copy-start.2
  1.7 1.0 copy-done.2
  2.7 0.0 copy-start.3
  2.7 1.0 copy-done.3
  3.8 0.0 copy-start.4
  3.8 1.0 copy-done.4
  4.8 0.0 copy-start.9
  4.8 0.9 copy-done.9
  5.7 0.0 copy-start.11
  5.7 0.7 copy-done.11
  6.4 0.0 copy-start.12
  6.4 0.7 copy-done.12
  7.1 0.0 copy-start.13
  7.1 0.7 copy-done.13
  7.8 6.8 %edges_and_grads.1 = (bf16[1024,256]{1,0:T(8,128)(2,1)S(1)}, bf16[256,1024]{1,0:T(8,128)(2,1)S(1)}, bf16[8,96,768]{2,1,0:T(8,128)(2,1)S(1)}) custom-call(bf16[1024,256]{1,0:T(8,128)(2,1)S(1)} %copy-done.1, bf16[1024,256]{1,0:T(8,128)(2,1)S(1)} %copy-done.2, bf16[1024,256]{1,0:T(8,128)(2,1)S(1)} %copy-done.3, bf16[1024,256]{1,0:T(8,128)(2,1)S(1)} %copy-done.4, ...), custom_call_target="tpu_custom_call" | custom-call | tf_op jit(solution)/shard_map/edges_and_grads/pallas_call | solution.py:140
  14.6 0.0 copy-start.5
  14.6 0.8 copy-done.5
  15.4 0.0 copy-start.7
  15.4 0.8 copy-done.7
  16.2 0.0 copy-start.10
  16.2 29.7 %all_to_all.27 = bf16[8,96,768]{2,1,0:T(8,128)(2,1)S(1)} all-to-all(bf16[8,96,768]{2,1,0:T(8,128)(2,1)S(1)} %get-tuple-element.8), channel_id=1, replica_groups=mesh['group'=96,'local'=8] {'local'}, dimensions={0} | all-to-all | bytes 2359296 | tf_op jit(solution)/shard_map/all_to_all | solution.py:170
  45.9 0.0 copy-start
  45.9 0.0 copy-start.15
  45.9 0.0 copy-start.16
  45.9 0.8 reduce_sum.12
  46.7 0.5 broadcast.5
  47.2 1.6 %reduce.2 = bf16[96,768]{1,0:T(8,128)(2,1)S(1)} reduce(bf16[96,1,768]{2,0,1:T(8,128)(2,1)} %bitcast.20, bf16[]{:T(256)} %broadcast.5), dimensions={1}, to_apply=%copy.16.reduce_sub_computation | reduce | bytes 294914 | tf_op jit(solution)/shard_map/all_to_all | solution.py:172
  48.8 0.7 reshape.40
  49.5 14.4 %all-to-all-start.1 = ((bf16[96,2,384]{2,1,0:T(2,128)(2,1)}), bf16[96,2,384]{2,1,0:T(2,128)(2,1)S(1)}, u32[]{:S(2)}, u32[]{:S(2)}) async-start(bf16[96,2,384]{2,1,0:T(2,128)(2,1)} %reshape.40), calls=%async_computation.1 | async-start | bytes 294912 | tf_op jit(solution)/shard_map/all_to_all | solution.py:172
  63.9 0.0 copy-done.10
  64.0 0.0 copy-done
  64.0 0.0 copy-done.15
  64.0 0.0 copy-done.16
  64.0 0.0 copy-start.6
  64.0 1.0 copy-done.6
  65.0 0.0 copy-start.8
  65.0 1.0 copy-done.8
  66.1 0.0 copy-start.14
  66.1 2.7 %tiles.1.base_ref = f32[1024,256]{1,0:T(8,128)S(1)} custom-call(s32[64]{0:T(128)S(1)} %copy-done.15, s32[64]{0:T(128)S(1)} %copy-done.16, bf16[64,128,128]{2,1,0:T(8,128)(2,1)S(1)} %copy-done, bf16[256,1024]{1,0:T(8,128)(2,1)S(1)} %copy-done.8, bf16[1024,256]{1,0:T(8,128)(2,1)S(1)} %copy-done.6, bf16[256,256]{1,0:T(8,128)(2,1)S(1)} %copy-done.10), custom_call_target="tpu_custom_call" | custom-call | tf_op jit(solution)/shard_map/tiles/pallas_call | solution.py:161
  68.8 9.7 %all-to-all-done.1 = bf16[96,2,384]{2,1,0:T(2,128)(2,1)S(1)} async-done(((bf16[96,2,384]{2,1,0:T(2,128)(2,1)}), bf16[96,2,384]{2,1,0:T(2,128)(2,1)S(1)}, u32[]{:S(2)}, u32[]{:S(2)}) %all-to-all-start.1) | async-done | bytes 147488 | tf_op jit(solution)/shard_map/all_to_all | solution.py:172
  78.4 0.1 reshape.41
  78.6 0.0 copy-done.14
  78.6 1.2 %finish.1 = (bf16[1024,256]{1,0:T(8,128)(2,1)}, bf16[1,256]{1,0:T(2,128)(2,1)S(1)}) custom-call(bf16[96,768]{1,0:T(8,128)(2,1)S(1)} %bitcast.15, s32[2,96]{1,0:T(2,128)S(1)} %bitcast.19, f32[1024,256]{1,0:T(8,128)S(1)} %tiles.1.base_ref), custom_call_target="tpu_custom_call" | custom-call | tf_op jit(solution)/shard_map/finish/pallas_call | solution.py:173
  79.8 0.1 broadcast_in_dim.6
  79.9 0.9 reduce.3
  80.8 18.5 %all_to_all.28 = bf16[96,2,128]{2,1,0:T(2,128)(2,1)S(1)} all-to-all(bf16[96,2,128]{2,1,0:T(2,128)(2,1)S(1)} %reshape.42), channel_id=1, replica_groups=mesh['group'=96,'local'=8] {'group'}, dimensions={0} | all-to-all | bytes 98304 | tf_op jit(solution)/shard_map/all_to_all | solution.py:182
  99.3 0.1 slice.15
  99.4 12.7 %all_to_all.29 = bf16[8,64,256]{2,1,0:T(8,128)(2,1)S(1)} all-to-all(bf16[8,64,256]{2,1,0:T(8,128)(2,1)S(1)} %broadcast_in_dim.15), channel_id=1, replica_groups=mesh['group'=96,'local'=8] {'local'}, dimensions={0} | all-to-all | bytes 524288 | tf_op jit(solution)/shard_map/all_to_all | solution.py:184
  112.1 0.8 fusion
  (6 shorter events, 0.1 us)
Async XLA Ops:
  0.6 1.0 copy-start.1
  1.7 1.0 copy-start.2
  2.7 1.0 copy-start.3
  3.8 1.0 copy-start.4
  4.8 0.9 copy-start.9
  5.7 0.7 copy-start.11
  6.4 0.7 copy-start.12
  7.1 0.7 copy-start.13
  14.6 0.8 copy-start.5
  15.4 0.8 copy-start.7
  16.2 47.8 %copy-start.10 = (bf16[256,256]{1,0:T(8,128)(2,1)S(1)}, bf16[256,256]{1,0:T(8,128)(2,1)}, u32[]{:S(2)}) copy-start(bf16[256,256]{1,0:T(8,128)(2,1)} %ws_ref.1) | copy-start | bytes 393220
  45.9 18.1 %copy-start = (bf16[64,128,128]{2,1,0:T(8,128)(2,1)S(1)}, bf16[64,128,128]{2,1,0:T(8,128)(2,1)}, u32[]{:S(2)}) copy-start(bf16[64,128,128]{2,1,0:T(8,128)(2,1)} %vals_ref.1) | copy-start | bytes 6291460
  45.9 18.1 %copy-start.15 = (s32[64]{0:T(128)S(1)}, s32[64]{0:T(128)}, u32[]{:S(2)}) copy-start(s32[64]{0:T(128)} %rows_ref.1) | copy-start | bytes 772
  45.9 18.1 %copy-start.16 = (s32[64]{0:T(128)S(1)}, s32[64]{0:T(128)}, u32[]{:S(2)}) copy-start(s32[64]{0:T(128)} %cols_ref.1) | copy-start | bytes 772
  49.5 28.9 %all-to-all-start.1 = ((bf16[96,2,384]{2,1,0:T(2,128)(2,1)}), bf16[96,2,384]{2,1,0:T(2,128)(2,1)S(1)}, u32[]{:S(2)}, u32[]{:S(2)}) async-start(bf16[96,2,384]{2,1,0:T(2,128)(2,1)} %reshape.40), calls=%async_computation.1 | async-start | bytes 294912 | tf_op jit(solution)/shard_map/all_to_all | solution.py:172
  64.0 1.0 copy-start.6
  65.0 1.0 copy-start.8
  66.1 12.5 %copy-start.14 = (s32[1,96,2]{1,2,0:T(2,128)S(1)}, s32[1,96,2]{1,2,0:T(2,128)}, u32[]{:S(2)}) copy-start(s32[1,96,2]{1,2,0:T(2,128)} %param.25) | copy-start | bytes 2308

commit v2 on v1

v2 whole, which is shorter than its diff:
```python
import jax
import jax.numpy as jnp
from jax import lax
from jax.experimental import pallas as pl
from jax.experimental.pallas import tpu as pltpu
from jax.sharding import PartitionSpec as P

F32 = jnp.float32
BF16 = jnp.bfloat16
VMEM_LIMIT = 24 * 1024 * 1024


def dot_nn(first_op, second_op):
    return lax.dot_general(first_op, second_op, (((1,), (0,)), ((), ())), preferred_element_type=F32)


def dot_nt(first_op, second_op):
    return lax.dot_general(first_op, second_op, (((1,), (1,)), ((), ())), preferred_element_type=F32)


def identity(size):
    row = lax.broadcasted_iota(jnp.int32, (size, size), 0)
    col = lax.broadcasted_iota(jnp.int32, (size, size), 1)
    return jnp.where(row == col, 1.0, 0.0).astype(BF16)


def edges_and_grads(groups, members, per_owner, scale, chunk):
    def kernel(
        preact_hbm, cot_hbm, wn_hbm, dst_hbm, slot_hbm, weight_hbm, feat_hbm, agg_hbm,
        dp_hbm, pushed_hbm, send_ref, keep_ref,
        preact_ref, cot_ref, wn_ref, dst_ref, slot_ref, weight_ref, feat_ref, agg_ref,
        dp_ref, pushed_ref, in_sem, out_sem,
    ):
        sources = (preact_hbm, cot_hbm, wn_hbm, dst_hbm, slot_hbm, weight_hbm, feat_hbm, agg_hbm)
        held = (preact_ref, cot_ref, wn_ref, dst_ref, slot_ref, weight_ref, feat_ref, agg_ref)
        loads = [pltpu.make_async_copy(s, d, in_sem.at[i]) for i, (s, d) in enumerate(zip(sources, held))]
        for load in loads:
            load.start()
        nodes, width = preact_ref.shape
        edges = dst_ref.shape[1]
        side = lax.rem(lax.axis_index("local"), 2)
        for load in loads[:6]:
            load.wait()
        x = preact_ref[...].astype(F32)
        sig = jax.nn.sigmoid(x)
        dp = (cot_ref[...].astype(F32) * sig * (1.0 + x * (1.0 - sig))).astype(BF16)
        dp_ref[...] = dp
        pushed_t = dot_nt(wn_ref[...], dp).astype(BF16)
        pushed_ref[...] = pushed_t
        stores = [
            pltpu.make_async_copy(dp_ref, dp_hbm, out_sem.at[0]),
            pltpu.make_async_copy(pushed_ref, pushed_hbm, out_sem.at[1]),
        ]
        for store in stores:
            store.start()

        all_terms = []
        for e0 in range(0, edges, chunk):
            dst = dst_ref[:, e0 : e0 + chunk]
            node = lax.broadcasted_iota(jnp.int32, (nodes, chunk), 0)
            take = jnp.where(node == dst, 1.0, 0.0).astype(BF16)
            all_terms.append((dot_nn(pushed_t, take) * weight_ref[:, e0 : e0 + chunk]).astype(BF16))
        terms = jnp.concatenate(all_terms, axis=1)

        slot = slot_ref[...]
        per_group = members * per_owner
        rows = members * groups
        group = slot // per_group
        rest = slot - group * per_group
        member = rest // per_owner
        which = rest - member * per_owner
        place = which * rows + member * groups + group
        for ref, parity in ((send_ref, 1 - side), (keep_ref, side)):
            for j in range(per_owner):
                for p in range(members // 2):
                    base = j * rows + (2 * p + parity) * groups
                    row = lax.broadcasted_iota(jnp.int32, (groups, edges), 0)
                    put = jnp.where(row == place - base, 1.0, 0.0).astype(BF16)
                    ref[p, :, j * width : (j + 1) * width] = dot_nt(put, terms).astype(BF16)

        for load in loads[6:]:
            load.wait()
        eye = identity(width)
        share = 2 * width // members
        empty = jnp.zeros((groups - share, width), BF16)
        lanes = slice(per_owner * width, (per_owner + 1) * width)
        for i, ref in enumerate((feat_ref, agg_ref)):
            grad = dot_nn(dot_nt(eye, ref[...]).astype(BF16), dp) * scale
            for k in range(members // 4):
                p = i * (members // 4) + k
                low = grad[2 * k * share : (2 * k + 1) * share]
                high = grad[(2 * k + 1) * share : (2 * k + 2) * share]
                send_ref[p, 0:share, lanes] = jnp.where(side == 0, high, low).astype(BF16)
                keep_ref[p, 0:share, lanes] = jnp.where(side == 0, low, high).astype(BF16)
                send_ref[p, share:, lanes] = empty
                keep_ref[p, share:, lanes] = empty
        for store in stores:
            store.wait()

    return kernel


def tiles_kernel(rows_ref, cols_ref, vals_ref, pushed_ref, dp_ref, ws_ref, out_ref, adj_ref):
    count, block, _ = vals_ref.shape
    adj_ref[...] = jnp.zeros_like(adj_ref)

    def add(t, carry):
        rows = pl.ds(pl.multiple_of(rows_ref[t] * block, block), block)
        cols = pl.ds(pl.multiple_of(cols_ref[t] * block, block), block)
        adj_ref[rows, cols] += vals_ref[t].astype(F32)
        return carry

    lax.fori_loop(0, count, add, 0)
    interior_t = dot_nn(pushed_ref[...], adj_ref[...].astype(BF16))
    out_ref[...] = dot_nt(dp_ref[...], ws_ref[...]) + interior_t.T


def finish_kernel(arrived_ref, target_ref, base_ref, out_ref):
    nodes, width = out_ref.shape
    groups = arrived_ref.shape[0]
    per_owner = target_ref.shape[0]
    arrived = arrived_ref[...]
    total = base_ref[...]
    for j in range(per_owner):
        node = lax.broadcasted_iota(jnp.int32, (nodes, groups), 0)
        put = jnp.where(node == target_ref[j : j + 1, :], 1.0, 0.0).astype(BF16)
        total += dot_nn(put, arrived[:, j * width : (j + 1) * width])
    out_ref[...] = total.astype(BF16)


def on_device(
    features,
    aggregate,
    preact,
    cotangent,
    w_self,
    w_neigh,
    tile_vals,
    tile_rows,
    tile_cols,
    edge_dst,
    edge_slot,
    edge_weight,
    recv_rows,
):
    groups = lax.axis_size("group")
    members = lax.axis_size("local")
    nodes, width = features.shape
    edges = edge_dst.shape[0]
    per_owner = recv_rows.shape[2]
    scale = (nodes * groups * members) ** (-0.5)
    payload = (per_owner + 1) * width
    share = 2 * width // members
    params = pltpu.CompilerParams(vmem_limit_bytes=VMEM_LIMIT)
    smem = pl.BlockSpec(memory_space=pltpu.SMEM)
    vmem = pl.BlockSpec(memory_space=pltpu.VMEM)
    hbm = pl.BlockSpec(memory_space=pltpu.HBM)

    operands = (
        preact,
        cotangent,
        w_neigh,
        edge_dst.reshape(1, edges),
        edge_slot.reshape(1, edges),
        edge_weight.reshape(1, edges),
        features,
        aggregate,
    )
    half = jax.ShapeDtypeStruct((members // 2, groups, payload), BF16)
    dp, pushed_t, send, keep = pl.pallas_call(
        edges_and_grads(groups, members, per_owner, scale, 512),
        out_shape=(
            jax.ShapeDtypeStruct((nodes, width), BF16),
            jax.ShapeDtypeStruct((width, nodes), BF16),
            half,
            half,
        ),
        in_specs=[hbm] * len(operands),
        out_specs=(hbm, hbm, vmem, vmem),
        scratch_shapes=[pltpu.VMEM(a.shape, a.dtype) for a in operands]
        + [
            pltpu.VMEM((nodes, width), BF16),
            pltpu.VMEM((width, nodes), BF16),
            pltpu.SemaphoreType.DMA((len(operands),)),
            pltpu.SemaphoreType.DMA((2,)),
        ],
        compiler_params=params,
        name="edges_and_grads",
    )(*[pltpu.with_memory_space_constraint(a, pltpu.HBM) for a in operands])
    base = pl.pallas_call(
        tiles_kernel,
        out_shape=jax.ShapeDtypeStruct((nodes, width), F32),
        in_specs=[smem, smem, vmem, vmem, vmem, vmem],
        out_specs=vmem,
        scratch_shapes=[pltpu.VMEM((nodes, nodes), F32)],
        compiler_params=params,
        name="tiles",
    )(tile_rows, tile_cols, tile_vals, pushed_t, dp, w_self)

    other_core = [(i, i ^ 1) for i in range(members)]
    along_x = [list(range(core, members, 2)) for core in range(2)]
    came = lax.ppermute(send, "local", other_core)
    chip_sum = (came.astype(F32) + keep.astype(F32)).astype(BF16)
    parts = lax.all_to_all(chip_sum, "local", 0, 0, axis_index_groups=along_x, tiled=True)
    summed = parts.astype(F32).sum(0).astype(BF16)
    arrived = lax.all_to_all(summed, "group", 0, 0, tiled=True)
    row = arrived[:, per_owner * width :].astype(F32).sum(0, keepdims=True).astype(BF16)
    spread = lax.all_to_all(jnp.broadcast_to(row, (groups, width)), "group", 0, 0, tiled=True)
    grad_x = pl.pallas_call(
        finish_kernel,
        out_shape=jax.ShapeDtypeStruct((nodes, width), BF16),
        compiler_params=params,
        name="finish",
    )(arrived, recv_rows.reshape(groups, per_owner).T, base)
    mine = spread[:share]
    grads = lax.all_to_all(jnp.broadcast_to(mine[None], (members, share, width)), "local", 0, 0, tiled=True)
    grads = grads.reshape(2, width, width).astype(F32)
    return (grad_x, grads[0], grads[1])


def solution(mesh):
    both = ("group", "local")
    placed = (
        P(both, None),
        P(both, None),
        P(both, None),
        P(both, None),
        P(),
        P(),
        P(both, None, None),
        P(both),
        P(both),
        P(both),
        P(both),
        P(both),
        P("group", None, "local"),
    )
    return jax.shard_map(
        on_device,
        mesh=mesh,
        in_specs=placed,
        out_specs=(P(both, None), P(), P()),
        check_vma=False,
    )
```

time: 114 us -> 108 us (0.947)
  local copies, waits for them, and re-layouts: 13.2 us -> 6.81 us
  starting transfers between devices: 14.4 us -> 20.6 us
  waiting for transfers between devices: 9.66 us -> 4.26 us
  Pallas kernels: 10.7 us -> 13.4 us
  blocking collectives: 60.8 us -> 59.4 us
    ppermute x0 -> x1, starting transfers between devices: none -> 12.4 us  [on_device(): came = lax.ppermute(send, 'local', other_core)]
    unnamed x40 -> x16, local copies, waits for them, and re-layouts: 11.7 us -> 3.65 us
    all_to_all x1, waiting for transfers between devices: 9.66 us -> 2.65 us  [on_device(): lax.all_to_all(jnp.broadcast_to(mine[None], (members, share, width)), 'lo...]
    all_to_all x1, starting transfers between devices: 14.4 us -> 8.2 us  [on_device(): lax.all_to_all(jnp.broadcast_to(mine[None], (members, share, width)), 'lo...]
    pallas_call x1, Pallas kernels: 6.8 us -> 9.44 us  [on_device(): pl.pallas_call(edges_and_grads(groups, members, per_owner, scale, 512), o...]
    all_to_all x2, blocking collectives: 42.4 us -> 40.2 us  [the longest x1 28.2 us: on_device(): arrived = lax.all_to_all(summed, 'group', 0, 0, tiled=True)]
    ppermute x0 -> x1, waiting for transfers between devices: none -> 1.61 us  [on_device(): came = lax.ppermute(send, 'local', other_core)]
  transfers between devices with their start and end apart: 1 -> 2, of which waited for: 1 -> 2; matrix products, arithmetic and copies ran while one was open for 0% -> 0% of each run, Pallas kernels for 2% -> 4%
where the time goes in v2:
time: 108 us
  blocking collectives  59.4 us (55%)
  starting transfers between devices  20.6 us (19%)
  Pallas kernels  13.4 us (12%)
  local copies, waits for them, and re-layouts  6.81 us (6%)
  waiting for transfers between devices  4.26 us (4%)
  other arithmetic  2.47 us (2%)
    all_to_all x1, blocking collectives, on_device(): arrived = lax.all_to_all(summed, 'group', 0, 0, tiled=True)  28.2 us
    all_to_all x1, blocking collectives, on_device(): lax.all_to_all(jnp.broadcast_to(row, (groups, width)), 'group', 0, 0, til...  19.2 us
    ppermute x1, starting transfers between devices, on_device(): came = lax.ppermute(send, 'local', other_core)  12.4 us
    all_to_all x1, blocking collectives, on_device(): lax.all_to_all(chip_sum, 'local', 0, 0, axis_index_groups=along_x, tiled=...  12 us
    pallas_call x1, Pallas kernels, on_device(): pl.pallas_call(edges_and_grads(groups, members, per_owner, scale, 512), o...  9.44 us
    all_to_all x1, starting transfers between devices, on_device(): lax.all_to_all(jnp.broadcast_to(mine[None], (members, share, width)), 'lo...  8.2 us
    unnamed x16, local copies, waits for them, and re-layouts  3.65 us
    pallas_call x1, Pallas kernels, on_device(): pl.pallas_call(tiles_kernel, out_shape=jax.ShapeDtypeStruct((nodes, width...  2.71 us
  transfers between devices with their start and end apart: 2, of which 2 were waited for; matrix products, arithmetic and copies ran while one was open for 0% of the time, Pallas kernels for 4%

profile of v2, /device:TPU:1, one launch (start us, length us, event | category | flops | bytes accessed | tf_op | source)
XLA Modules:
  0.0 107.7 jit_solution(8778763770384389618)
XLA Ops:
  0.6 9.4 %edges_and_grads.1 = (bf16[1024,256]{1,0:T(8,128)(2,1)S(1)}, bf16[256,1024]{1,0:T(8,128)(2,1)S(1)}, bf16[4,96,768]{2,1,0:T(8,128)(2,1)S(1)}, bf16[4,96,768]{2,1,0:T(8,128)(2,1)S(1)}) custom-call(bf16[1024,256]{1,0:T(8,128)(2,1)} %preact_hbm.1, bf16[1024,256]{1,0:T(8,128)(2,1)} %cot_hbm.1, bf16[256,256]{1,0:T(8,128)(2,1)} %wn_hbm.1, s32[1,2048]{1,0:T(1,128)} %bitcast.22, ...), custom_call_target="tpu_custom_call" | custom-call | tf_op jit(solution)/shard_map/edges_and_grads/pallas_call | solution.py:170
  10.1 12.4 %collective-permute-start = (bf16[4,96,768]{2,1,0:T(8,128)(2,1)S(1)}, bf16[4,96,768]{2,1,0:T(8,128)(2,1)S(1)}, u32[]{:S(2)}, u32[]{:S(2)}) collective-permute-start(bf16[4,96,768]{2,1,0:T(8,128)(2,1)S(1)} %get-tuple-element.7), channel_id=1, source_target_pairs={{0,1},{1,0},{2,3},{3,2},{4,5},{5,4},{6,7},{7,6},{8,9},{9,8},{10,11... | collective-permute-start | bytes 1769480 | tf_op jit(solution)/shard_map/ppermute | solution.py:202
  22.5 1.6 %collective-permute-done = bf16[4,96,768]{2,1,0:T(8,128)(2,1)S(1)} collective-permute-done((bf16[4,96,768]{2,1,0:T(8,128)(2,1)S(1)}, bf16[4,96,768]{2,1,0:T(8,128)(2,1)S(1)}, u32[]{:S(2)}, u32[]{:S(2)}) %collective-permute-start) | collective-permute-done | bytes 589856 | tf_op jit(solution)/shard_map/ppermute | solution.py:202
  24.1 0.1 add_convert_fusion
  24.3 12.0 %all_to_all.27 = bf16[4,96,768]{2,1,0:T(8,128)(2,1)S(1)} all-to-all(bf16[4,96,768]{2,1,0:T(8,128)(2,1)S(1)} %add_convert_fusion), channel_id=1, replica_groups={{0,2,4,6},{1,3,5,7},{8,10,12,14},{9,11,13,15},{16,18,20,22},{17,19,21,2..., dimensions={0} | all-to-all | bytes 1179648 | tf_op jit(solution)/shard_map/all_to_all | solution.py:204
  36.3 0.1 reduce_sum.24
  36.4 0.5 broadcast.4
  36.9 0.7 reduce.2
  37.6 28.2 %all_to_all.28 = bf16[96,2,384]{2,1,0:T(2,128)(2,1)S(1)} all-to-all(bf16[96,2,384]{2,1,0:T(2,128)(2,1)S(1)} %reshape.43), channel_id=1, replica_groups=mesh['group'=96,'local'=8] {'group'}, dimensions={0} | all-to-all | bytes 294912 | tf_op jit(solution)/shard_map/all_to_all | solution.py:206
  65.8 0.0 copy-start.1
  65.8 0.8 reshape.44
  66.6 0.0 copy-start
  66.6 0.0 copy-start.3
  66.6 0.0 copy-start.4
  66.6 1.1 %copy.22 = bf16[96,1,768]{2,0,1:T(8,128)(2,1)S(1)} copy(bf16[96,1,768]{2,1,0:T(2,128)(2,1)} %reshape.44) | data formatting | bytes 294912
  67.8 0.1 broadcast_in_dim.6
  67.8 1.5 %reduce.3 = bf16[96,256]{1,0:T(8,128)(2,1)} reduce(bf16[96,1,256]{2,1,0:T(2,128)(2,1)S(1)} %broadcast_in_dim.6, bf16[]{:T(256)} %broadcast.4), dimensions={1}, to_apply=%broadcast_in_dim.6.reduce_sub_computation | reduce | bytes 98306 | tf_op jit(solution)/shard_map/broadcast_in_dim | solution.py:208
  69.4 0.8 reshape.45
  70.2 19.2 %all_to_all.29 = bf16[96,2,128]{2,1,0:T(2,128)(2,1)} all-to-all(bf16[96,2,128]{2,1,0:T(2,128)(2,1)S(1)} %reshape.45), channel_id=1, replica_groups=mesh['group'=96,'local'=8] {'group'}, dimensions={0} | all-to-all | bytes 98304 | tf_op jit(solution)/shard_map/all_to_all | solution.py:208
  89.4 0.8 reshape.46
  90.2 0.1 slice.20
  90.3 0.7 broadcast_in_dim.16
  91.0 8.2 %all-to-all-start.3 = ((bf16[8,64,256]{2,1,0:T(8,128)(2,1)}), bf16[8,64,256]{2,1,0:T(8,128)(2,1)}, u32[]{:S(2)}, u32[]{:S(2)}) async-start(bf16[8,64,256]{2,1,0:T(8,128)(2,1)} %broadcast_in_dim.16), calls=%async_computation.3 | async-start | bytes 524288 | tf_op jit(solution)/shard_map/all_to_all | solution.py:216
  99.2 0.0 copy-done.1
  99.3 0.0 copy-done
  99.3 0.0 copy-done.3
  99.3 0.0 copy-done.4
  99.3 0.0 copy-start.2
  99.3 2.7 %tiles.1.base_ref = f32[1024,256]{1,0:T(8,128)S(1)} custom-call(s32[64]{0:T(128)S(1)} %copy-done.3, s32[64]{0:T(128)S(1)} %copy-done.4, bf16[64,128,128]{2,1,0:T(8,128)(2,1)S(1)} %copy-done, bf16[256,1024]{1,0:T(8,128)(2,1)S(1)} %get-tuple-element.9.pushed_ref, bf16[1024,256]{1,0:T(8,128)(2,1)S(1)} %get-tuple-element.10.dp_ref, bf16[256,256]{1,0:T(8,128)(2,1)S(1)} %copy-done.1), custom_call_target="tpu_custom_call" | custom-call | tf_op jit(solution)/shard_map/tiles/pallas_call | solution.py:190
  102.0 0.0 copy-done.2
  102.0 1.2 %finish.1 = bf16[1024,256]{1,0:T(8,128)(2,1)} custom-call(bf16[96,768]{1,0:T(8,128)(2,1)S(1)} %bitcast.16, s32[2,96]{1,0:T(2,128)S(1)} %bitcast.17, f32[1024,256]{1,0:T(8,128)S(1)} %tiles.1.base_ref), custom_call_target="tpu_custom_call" | custom-call | tf_op jit(solution)/shard_map/finish/pallas_call | solution.py:209
  103.2 2.6 %all-to-all-done.3 = bf16[8,64,256]{2,1,0:T(8,128)(2,1)} async-done(((bf16[8,64,256]{2,1,0:T(8,128)(2,1)}), bf16[8,64,256]{2,1,0:T(8,128)(2,1)}, u32[]{:S(2)}, u32[]{:S(2)}) %all-to-all-start.3) | async-done | bytes 262176 | tf_op jit(solution)/shard_map/all_to_all | solution.py:216
  105.9 1.8 %fusion = (f32[4,64,256]{2,1,0:T(8,128)}, f32[4,64,256]{2,1,0:T(8,128)}) fusion(bf16[8,64,256]{2,1,0:T(8,128)(2,1)} %all-to-all-done.3), kind=kLoop, calls=%fused_computation.4 | loop fusion | bytes 1048576 | tf_op jit(solution)/shard_map/slice | solution.py:218
  (3 shorter events, 0.1 us)
Async XLA Ops:
  10.1 14.0 %collective-permute-start = (bf16[4,96,768]{2,1,0:T(8,128)(2,1)S(1)}, bf16[4,96,768]{2,1,0:T(8,128)(2,1)S(1)}, u32[]{:S(2)}, u32[]{:S(2)}) collective-permute-start(bf16[4,96,768]{2,1,0:T(8,128)(2,1)S(1)} %get-tuple-element.7), channel_id=1, source_target_pairs={{0,1},{1,0},{2,3},{3,2},{4,5},{5,4},{6,7},{7,6},{8,9},{9,8},{10,11... | collective-permute-start | bytes 1769480 | tf_op jit(solution)/shard_map/ppermute | solution.py:202
  65.8 33.5 %copy-start.1 = (bf16[256,256]{1,0:T(8,128)(2,1)S(1)}, bf16[256,256]{1,0:T(8,128)(2,1)}, u32[]{:S(2)}) copy-start(bf16[256,256]{1,0:T(8,128)(2,1)} %ws_ref.1) | copy-start | bytes 393220
  66.6 32.7 %copy-start = (bf16[64,128,128]{2,1,0:T(8,128)(2,1)S(1)}, bf16[64,128,128]{2,1,0:T(8,128)(2,1)}, u32[]{:S(2)}) copy-start(bf16[64,128,128]{2,1,0:T(8,128)(2,1)} %vals_ref.1) | copy-start | bytes 6291460
  66.6 32.7 %copy-start.3 = (s32[64]{0:T(128)S(1)}, s32[64]{0:T(128)}, u32[]{:S(2)}) copy-start(s32[64]{0:T(128)} %rows_ref.1) | copy-start | bytes 772
  66.6 32.7 %copy-start.4 = (s32[64]{0:T(128)S(1)}, s32[64]{0:T(128)}, u32[]{:S(2)}) copy-start(s32[64]{0:T(128)} %cols_ref.1) | copy-start | bytes 772
  91.0 14.8 %all-to-all-start.3 = ((bf16[8,64,256]{2,1,0:T(8,128)(2,1)}), bf16[8,64,256]{2,1,0:T(8,128)(2,1)}, u32[]{:S(2)}, u32[]{:S(2)}) async-start(bf16[8,64,256]{2,1,0:T(8,128)(2,1)} %broadcast_in_dim.16), calls=%async_computation.3 | async-start | bytes 524288 | tf_op jit(solution)/shard_map/all_to_all | solution.py:216
  99.3 2.7 %copy-start.2 = (s32[1,96,2]{1,2,0:T(2,128)S(1)}, s32[1,96,2]{1,2,0:T(2,128)}, u32[]{:S(2)}) copy-start(s32[1,96,2]{1,2,0:T(2,128)} %param.25) | copy-start | bytes 2308

commit v3 on v2

--- a/solution.py
+++ b/solution.py
@@ -26,20 +26,39 @@
 
 def edges_and_grads(groups, members, per_owner, scale, chunk):
     def kernel(
-        preact_hbm, cot_hbm, wn_hbm, dst_hbm, slot_hbm, weight_hbm, feat_hbm, agg_hbm,
+        dst_hbm, slot_hbm, weight_hbm, preact_hbm, cot_hbm, wn_hbm, feat_hbm, agg_hbm,
         dp_hbm, pushed_hbm, send_ref, keep_ref,
-        preact_ref, cot_ref, wn_ref, dst_ref, slot_ref, weight_ref, feat_ref, agg_ref,
-        dp_ref, pushed_ref, in_sem, out_sem,
+        dst_ref, slot_ref, weight_ref, preact_ref, cot_ref, wn_ref, feat_ref, agg_ref,
+        dp_ref, pushed_ref, put_ref, in_sem, out_sem,
     ):
-        sources = (preact_hbm, cot_hbm, wn_hbm, dst_hbm, slot_hbm, weight_hbm, feat_hbm, agg_hbm)
-        held = (preact_ref, cot_ref, wn_ref, dst_ref, slot_ref, weight_ref, feat_ref, agg_ref)
+        sources = (dst_hbm, slot_hbm, weight_hbm, preact_hbm, cot_hbm, wn_hbm, feat_hbm, agg_hbm)
+        held = (dst_ref, slot_ref, weight_ref, preact_ref, cot_ref, wn_ref, feat_ref, agg_ref)
         loads = [pltpu.make_async_copy(s, d, in_sem.at[i]) for i, (s, d) in enumerate(zip(sources, held))]
         for load in loads:
             load.start()
         nodes, width = preact_ref.shape
         edges = dst_ref.shape[1]
         side = lax.rem(lax.axis_index("local"), 2)
-        for load in loads[:6]:
+        for load in loads[:3]:
+            load.wait()
+        slot = slot_ref[...]
+        per_group = members * per_owner
+        rows = members * groups
+        group = slot // per_group
+        rest = slot - group * per_group
+        member = rest // per_owner
+        which = rest - member * per_owner
+        place = which * rows + member * groups + group
+        row = lax.broadcasted_iota(jnp.int32, (groups, edges), 0)
+        pieces = [
+            (ref, j, p, j * rows + (2 * p + parity) * groups)
+            for ref, parity in ((send_ref, 1 - side), (keep_ref, side))
+            for j in range(per_owner)
+            for p in range(members // 2)
+        ]
+        for n, (_, _, _, first) in enumerate(pieces):
+            put_ref[n] = jnp.where(row == place - first, 1.0, 0.0).astype(BF16)
+        for load in loads[3:6]:
             load.wait()
         x = preact_ref[...].astype(F32)
         sig = jax.nn.sigmoid(x)
@@ -62,21 +81,8 @@
             all_terms.append((dot_nn(pushed_t, take) * weight_ref[:, e0 : e0 + chunk]).astype(BF16))
         terms = jnp.concatenate(all_terms, axis=1)
 
-        slot = slot_ref[...]
-        per_group = members * per_owner
-        rows = members * groups
-        group = slot // per_group
-        rest = slot - group * per_group
-        member = rest // per_owner
-        which = rest - member * per_owner
-        place = which * rows + member * groups + group
-        for ref, parity in ((send_ref, 1 - side), (keep_ref, side)):
-            for j in range(per_owner):
-                for p in range(members // 2):
-                    base = j * rows + (2 * p + parity) * groups
-                    row = lax.broadcasted_iota(jnp.int32, (groups, edges), 0)
-                    put = jnp.where(row == place - base, 1.0, 0.0).astype(BF16)
-                    ref[p, :, j * width : (j + 1) * width] = dot_nt(put, terms).astype(BF16)
+        for n, (ref, j, p, _) in enumerate(pieces):
+            ref[p, :, j * width : (j + 1) * width] = dot_nt(put_ref[n], terms).astype(BF16)
 
         for load in loads[6:]:
             load.wait()
@@ -115,17 +121,40 @@
     out_ref[...] = dot_nt(dp_ref[...], ws_ref[...]) + interior_t.T
 
 
+def member_sum_kernel(parts_ref, out_ref):
+    total = jnp.sum(parts_ref[...].astype(F32), axis=0)
+    half = out_ref.shape[2]
+    out_ref[:, 0, :] = total[:, :half].astype(BF16)
+    out_ref[:, 1, :] = total[:, half:].astype(BF16)
+
+
+def grad_row_kernel(arrived_ref, out_ref):
+    half = out_ref.shape[2]
+    row = jnp.sum(arrived_ref[:, 1, half:].astype(F32), axis=0, keepdims=True).astype(BF16)
+    for k in range(2):
+        out_ref[:, k, :] = jnp.broadcast_to(row[:, k * half : (k + 1) * half], (out_ref.shape[0], half))
+
+
 def finish_kernel(arrived_ref, target_ref, base_ref, out_ref):
     nodes, width = out_ref.shape
     groups = arrived_ref.shape[0]
     per_owner = target_ref.shape[0]
-    arrived = arrived_ref[...]
+    arrived = jnp.concatenate([arrived_ref[:, 0, :], arrived_ref[:, 1, :]], axis=1)
     total = base_ref[...]
     for j in range(per_owner):
         node = lax.broadcasted_iota(jnp.int32, (nodes, groups), 0)
         put = jnp.where(node == target_ref[j : j + 1, :], 1.0, 0.0).astype(BF16)
         total += dot_nn(put, arrived[:, j * width : (j + 1) * width])
     out_ref[...] = total.astype(BF16)
+
+
+def widen_kernel(grads_ref, self_ref, neigh_ref):
+    members, share, _, half = grads_ref.shape
+    for m in range(members):
+        ref = (self_ref, neigh_ref)[2 * m // members]
+        first = m % (members // 2) * share
+        for k in range(2):
+            ref[first : first + share, k * half : (k + 1) * half] = grads_ref[m, :, k, :].astype(F32)
 
 
 def on_device(
@@ -157,12 +186,12 @@
     hbm = pl.BlockSpec(memory_space=pltpu.HBM)
 
     operands = (
+        edge_dst.reshape(1, edges),
+        edge_slot.reshape(1, edges),
+        edge_weight.reshape(1, edges),
         preact,
         cotangent,
         w_neigh,
-        edge_dst.reshape(1, edges),
-        edge_slot.reshape(1, edges),
-        edge_weight.reshape(1, edges),
         features,
         aggregate,
     )
@@ -170,8 +199,8 @@
     dp, pushed_t, send, keep = pl.pallas_call(
         edges_and_grads(groups, members, per_owner, scale, 512),
         out_shape=(
-            jax.ShapeDtypeStruct((nodes, width), BF16),
-            jax.ShapeDtypeStruct((width, nodes), BF16),
+            pltpu.HBM((nodes, width), BF16),
+            pltpu.HBM((width, nodes), BF16),
             half,
             half,
         ),
@@ -181,6 +210,7 @@
         + [
             pltpu.VMEM((nodes, width), BF16),
             pltpu.VMEM((width, nodes), BF16),
+            pltpu.VMEM((members * per_owner, groups, edges), BF16),
             pltpu.SemaphoreType.DMA((len(operands),)),
             pltpu.SemaphoreType.DMA((2,)),
         ],
@@ -202,20 +232,37 @@
     came = lax.ppermute(send, "local", other_core)
     chip_sum = (came.astype(F32) + keep.astype(F32)).astype(BF16)
     parts = lax.all_to_all(chip_sum, "local", 0, 0, axis_index_groups=along_x, tiled=True)
-    summed = parts.astype(F32).sum(0).astype(BF16)
+    summed = pl.pallas_call(
+        member_sum_kernel,
+        out_shape=jax.ShapeDtypeStruct((groups, 2, payload // 2), BF16),
+        compiler_params=params,
+        name="member_sum",
+    )(parts)
     arrived = lax.all_to_all(summed, "group", 0, 0, tiled=True)
-    row = arrived[:, per_owner * width :].astype(F32).sum(0, keepdims=True).astype(BF16)
-    spread = lax.all_to_all(jnp.broadcast_to(row, (groups, width)), "group", 0, 0, tiled=True)
+    rows = pl.pallas_call(
+        grad_row_kernel,
+        out_shape=jax.ShapeDtypeStruct((groups, 2, width // 2), BF16),
+        compiler_params=params,
+        name="grad_row",
+    )(arrived)
+    rows, base = lax.optimization_barrier((rows, base))
+    spread = lax.all_to_all(rows, "group", 0, 0, tiled=True)
     grad_x = pl.pallas_call(
         finish_kernel,
         out_shape=jax.ShapeDtypeStruct((nodes, width), BF16),
         compiler_params=params,
         name="finish",
     )(arrived, recv_rows.reshape(groups, per_owner).T, base)
-    mine = spread[:share]
-    grads = lax.all_to_all(jnp.broadcast_to(mine[None], (members, share, width)), "local", 0, 0, tiled=True)
-    grads = grads.reshape(2, width, width).astype(F32)
-    return (grad_x, grads[0], grads[1])
+    spread, grad_x = lax.optimization_barrier((spread, grad_x))
+    mine = jnp.broadcast_to(spread[None, :share], (members, share, 2, width // 2))
+    grads = lax.all_to_all(mine, "local", 0, 0, tiled=True)
+    grad_self, grad_neigh = pl.pallas_call(
+        widen_kernel,
+        out_shape=(jax.ShapeDtypeStruct((width, width), F32), jax.ShapeDtypeStruct((width, width), F32)),
+        compiler_params=params,
+        name="widen",
+    )(grads)
+    return (grad_x, grad_self, grad_neigh)
 
 
 def solution(mesh):

time: 108 us -> 101 us (0.935)
  blocking collectives: 59.4 us -> 25.5 us
  waiting for transfers between devices: 4.26 us -> 22.4 us
  starting transfers between devices: 20.6 us -> 32.5 us
  local copies, waits for them, and re-layouts: 6.81 us -> 2.27 us
  Pallas kernels: 13.4 us -> 16.6 us
  other arithmetic: 2.47 us -> 0.14 us
    all_to_all x2 -> x1, blocking collectives: 47.4 us -> 13.4 us  [on_device(): grads = lax.all_to_all(mine, 'local', 0, 0, tiled=True)]
    all_to_all x1 -> x2, waiting for transfers between devices: 2.65 us -> 20.8 us  [the longest x1 11.4 us: on_device(): spread = lax.all_to_all(rows, 'group', 0, 0, tiled=True)]
    all_to_all x1 -> x2, starting transfers between devices: 8.2 us -> 20 us  [the longest x1 14.1 us: on_device(): arrived = lax.all_to_all(summed, 'group', 0, 0, tiled=True)]
    pallas_call x0 -> x3, Pallas kernels: none -> 2.92 us  [the longest x1 1.24 us: on_device(): pl.pallas_call(widen_kernel, out_shape=(jax.ShapeDtypeStruct((width, widt...]
    slice x2 -> x1, local copies, waits for them, and re-layouts: 1.87 us -> 0.02 us  [on_device(): spread[None, :share]]
    unnamed x16 -> x14, local copies, waits for them, and re-layouts: 3.65 us -> 2.1 us
    broadcast_in_dim x1 -> x0, other arithmetic: 1.53 us -> none  [on_device(): jnp.broadcast_to(row, (groups, width))]
  transfers between devices with their start and end apart: 2 -> 3, of which waited for: 2 -> 3; matrix products, arithmetic and copies ran while one was open for 0% -> 0% of each run, Pallas kernels for 4% -> 4%
where the time goes in v3:
time: 101 us; the launch traced here: 100 us
  starting transfers between devices  32.5 us (32%)
  blocking collectives  25.5 us (25%)
  waiting for transfers between devices  22.4 us (22%)
  Pallas kernels  16.6 us (16%)
  local copies, waits for them, and re-layouts  2.27 us (2%)
    all_to_all x1, starting transfers between devices, on_device(): arrived = lax.all_to_all(summed, 'group', 0, 0, tiled=True)  14.1 us
    all_to_all x1, blocking collectives, on_device(): grads = lax.all_to_all(mine, 'local', 0, 0, tiled=True)  13.4 us
    ppermute x1, starting transfers between devices, on_device(): came = lax.ppermute(send, 'local', other_core)  12.4 us
    all_to_all x1, blocking collectives, on_device(): lax.all_to_all(chip_sum, 'local', 0, 0, axis_index_groups=along_x, tiled=...  12.2 us
    all_to_all x1, waiting for transfers between devices, on_device(): spread = lax.all_to_all(rows, 'group', 0, 0, tiled=True)  11.4 us
    pallas_call x1, Pallas kernels, on_device(): pl.pallas_call(edges_and_grads(groups, members, per_owner, scale, 512), o...  9.47 us
    all_to_all x1, waiting for transfers between devices, on_device(): arrived = lax.all_to_all(summed, 'group', 0, 0, tiled=True)  9.4 us
    all_to_all x1, starting transfers between devices, on_device(): spread = lax.all_to_all(rows, 'group', 0, 0, tiled=True)  5.91 us
  transfers between devices with their start and end apart: 3, of which 3 were waited for; matrix products, arithmetic and copies ran while one was open for 0% of the time, Pallas kernels for 4%

profile of v3, /device:TPU:1, one launch (start us, length us, event | category | flops | bytes accessed | tf_op | source)
XLA Modules:
  0.0 100.2 jit_solution(18116586829875460137)
XLA Ops:
  0.6 9.5 %edges_and_grads.1 = (bf16[1024,256]{1,0:T(8,128)(2,1)}, bf16[256,1024]{1,0:T(8,128)(2,1)}, bf16[4,96,768]{2,1,0:T(8,128)(2,1)S(1)}, bf16[4,96,768]{2,1,0:T(8,128)(2,1)S(1)}) custom-call(s32[1,2048]{1,0:T(1,128)} %bitcast.7, s32[1,2048]{1,0:T(1,128)} %bitcast.8, f32[1,2048]{1,0:T(1,128)} %bitcast.9, bf16[1024,256]{1,0:T(8,128)(2,1)} %preact_hbm.1, ...), custom_call_target="tpu_custom_call" | custom-call | tf_op jit(solution)/shard_map/edges_and_grads/pallas_call | solution.py:199
  10.1 12.4 %collective-permute-start = (bf16[4,96,768]{2,1,0:T(8,128)(2,1)S(1)}, bf16[4,96,768]{2,1,0:T(8,128)(2,1)S(1)}, u32[]{:S(2)}, u32[]{:S(2)}) collective-permute-start(bf16[4,96,768]{2,1,0:T(8,128)(2,1)S(1)} %get-tuple-element.13), channel_id=1, source_target_pairs={{0,1},{1,0},{2,3},{3,2},{4,5},{5,4},{6,7},{7,6},{8,9},{9,8},{10,11... | collective-permute-start | bytes 1769480 | tf_op jit(solution)/shard_map/ppermute | solution.py:232
  22.5 1.6 %collective-permute-done = bf16[4,96,768]{2,1,0:T(8,128)(2,1)S(1)} collective-permute-done((bf16[4,96,768]{2,1,0:T(8,128)(2,1)S(1)}, bf16[4,96,768]{2,1,0:T(8,128)(2,1)S(1)}, u32[]{:S(2)}, u32[]{:S(2)}) %collective-permute-start) | collective-permute-done | bytes 589856 | tf_op jit(solution)/shard_map/ppermute | solution.py:232
  24.2 0.0 copy-start.3
  24.2 0.1 add_convert_fusion
  24.3 0.0 copy-start
  24.3 0.0 copy-start.5
  24.3 0.0 copy-start.6
  24.3 12.2 %all_to_all.20.parts_ref = bf16[4,96,768]{2,1,0:T(8,128)(2,1)S(1)} all-to-all(bf16[4,96,768]{2,1,0:T(8,128)(2,1)S(1)} %add_convert_fusion), channel_id=1, replica_groups={{0,2,4,6},{1,3,5,7},{8,10,12,14},{9,11,13,15},{16,18,20,22},{17,19,21,2..., dimensions={0} | all-to-all | bytes 1179648 | tf_op jit(solution)/shard_map/all_to_all | solution.py:234
  36.5 0.9 member_sum.1
  37.4 14.1 %all-to-all-start.1 = ((bf16[96,2,384]{2,1,0:T(2,128)(2,1)}), bf16[96,2,384]{2,1,0:T(2,128)(2,1)S(1)}, u32[]{:S(2)}, u32[]{:S(2)}) async-start(bf16[96,2,384]{2,1,0:T(2,128)(2,1)} %member_sum.1), calls=%async_computation.1 | async-start | bytes 294912 | tf_op jit(solution)/shard_map/all_to_all | solution.py:241
  51.5 0.0 copy-done.3
  51.5 0.0 copy-done
  51.5 0.0 copy-done.5
  51.5 0.0 copy-done.6
  51.6 0.0 copy-start.1
  51.6 1.0 %copy-done.1 = bf16[1024,256]{1,0:T(8,128)(2,1)S(1)} copy-done((bf16[1024,256]{1,0:T(8,128)(2,1)S(1)}, bf16[1024,256]{1,0:T(8,128)(2,1)}, u32[]{:S(2)}) %copy-start.1) | copy-done | bytes 524312
  52.6 0.0 copy-start.2
  52.6 1.0 %copy-done.2 = bf16[256,1024]{1,0:T(8,128)(2,1)S(1)} copy-done((bf16[256,1024]{1,0:T(8,128)(2,1)S(1)}, bf16[256,1024]{1,0:T(8,128)(2,1)}, u32[]{:S(2)}) %copy-start.2) | copy-done | bytes 524312
  53.6 0.0 copy-start.4
  53.6 2.7 %tiles.1.base_ref = f32[1024,256]{1,0:T(8,128)S(1)} custom-call(s32[64]{0:T(128)S(1)} %copy-done.5, s32[64]{0:T(128)S(1)} %copy-done.6, bf16[64,128,128]{2,1,0:T(8,128)(2,1)S(1)} %copy-done, bf16[256,1024]{1,0:T(8,128)(2,1)S(1)} %copy-done.2, bf16[1024,256]{1,0:T(8,128)(2,1)S(1)} %copy-done.1, bf16[256,256]{1,0:T(8,128)(2,1)S(1)} %copy-done.3), custom_call_target="tpu_custom_call" | custom-call | tf_op jit(solution)/shard_map/tiles/pallas_call | solution.py:220
  56.4 9.4 %all-to-all-done.1.arrived_ref = bf16[96,2,384]{2,1,0:T(2,128)(2,1)S(1)} async-done(((bf16[96,2,384]{2,1,0:T(2,128)(2,1)}), bf16[96,2,384]{2,1,0:T(2,128)(2,1)S(1)}, u32[]{:S(2)}, u32[]{:S(2)}) %all-to-all-start.1) | async-done | bytes 147488 | tf_op jit(solution)/shard_map/all_to_all | solution.py:241
  65.8 0.8 grad_row.1
  66.5 5.9 %all-to-all-start.2 = ((bf16[96,2,128]{2,1,0:T(2,128)(2,1)}), bf16[96,2,128]{2,1,0:T(2,128)(2,1)S(1)}, u32[]{:S(2)}, u32[]{:S(2)}) async-start(bf16[96,2,128]{2,1,0:T(2,128)(2,1)} %grad_row.1), calls=%async_computation.2 | async-start | bytes 98304 | tf_op jit(solution)/shard_map/all_to_all | solution.py:249
  72.4 0.0 copy-done.4
  72.5 1.5 %finish.1 = bf16[1024,256]{1,0:T(8,128)(2,1)} custom-call(bf16[96,2,384]{2,1,0:T(2,128)(2,1)S(1)} %all-to-all-done.1.arrived_ref, s32[2,96]{1,0:T(2,128)S(1)} %bitcast.6, f32[1024,256]{1,0:T(8,128)S(1)} %tiles.1.base_ref), custom_call_target="tpu_custom_call" | custom-call | tf_op jit(solution)/shard_map/finish/pallas_call | solution.py:250
  74.0 11.4 %all-to-all-done.2 = bf16[96,2,128]{2,1,0:T(2,128)(2,1)S(1)} async-done(((bf16[96,2,128]{2,1,0:T(2,128)(2,1)}), bf16[96,2,128]{2,1,0:T(2,128)(2,1)S(1)}, u32[]{:S(2)}, u32[]{:S(2)}) %all-to-all-start.2) | async-done | bytes 49184 | tf_op jit(solution)/shard_map/all_to_all | solution.py:249
  85.4 0.1 broadcast_in_dim.2
  85.5 13.4 %all_to_all.21.grads_ref = bf16[8,64,2,128]{3,2,1,0:T(2,128)(2,1)S(1)} all-to-all(bf16[8,64,2,128]{3,2,1,0:T(2,128)(2,1)S(1)} %broadcast_in_dim.2), channel_id=1, replica_groups=mesh['group'=96,'local'=8] {'local'}, dimensions={0} | all-to-all | bytes 524288 | tf_op jit(solution)/shard_map/all_to_all | solution.py:258
  98.9 1.2 %widen.1 = (f32[256,256]{1,0:T(8,128)}, f32[256,256]{1,0:T(8,128)}) custom-call(bf16[8,64,2,128]{3,2,1,0:T(2,128)(2,1)S(1)} %all_to_all.21.grads_ref), custom_call_target="tpu_custom_call" | custom-call | tf_op jit(solution)/shard_map/widen/pallas_call | solution.py:259
  (1 shorter events, 0.0 us)
Async XLA Ops:
  10.1 14.0 %collective-permute-start = (bf16[4,96,768]{2,1,0:T(8,128)(2,1)S(1)}, bf16[4,96,768]{2,1,0:T(8,128)(2,1)S(1)}, u32[]{:S(2)}, u32[]{:S(2)}) collective-permute-start(bf16[4,96,768]{2,1,0:T(8,128)(2,1)S(1)} %get-tuple-element.13), channel_id=1, source_target_pairs={{0,1},{1,0},{2,3},{3,2},{4,5},{5,4},{6,7},{7,6},{8,9},{9,8},{10,11... | collective-permute-start | bytes 1769480 | tf_op jit(solution)/shard_map/ppermute | solution.py:232
  24.2 27.4 %copy-start.3 = (bf16[256,256]{1,0:T(8,128)(2,1)S(1)}, bf16[256,256]{1,0:T(8,128)(2,1)}, u32[]{:S(2)}) copy-start(bf16[256,256]{1,0:T(8,128)(2,1)} %ws_ref.1) | copy-start | bytes 393220
  24.3 27.2 %copy-start = (bf16[64,128,128]{2,1,0:T(8,128)(2,1)S(1)}, bf16[64,128,128]{2,1,0:T(8,128)(2,1)}, u32[]{:S(2)}) copy-start(bf16[64,128,128]{2,1,0:T(8,128)(2,1)} %vals_ref.1) | copy-start | bytes 6291460
  24.3 27.2 %copy-start.5 = (s32[64]{0:T(128)S(1)}, s32[64]{0:T(128)}, u32[]{:S(2)}) copy-start(s32[64]{0:T(128)} %rows_ref.1) | copy-start | bytes 772
  24.3 27.2 %copy-start.6 = (s32[64]{0:T(128)S(1)}, s32[64]{0:T(128)}, u32[]{:S(2)}) copy-start(s32[64]{0:T(128)} %cols_ref.1) | copy-start | bytes 772
  37.4 28.4 %all-to-all-start.1 = ((bf16[96,2,384]{2,1,0:T(2,128)(2,1)}), bf16[96,2,384]{2,1,0:T(2,128)(2,1)S(1)}, u32[]{:S(2)}, u32[]{:S(2)}) async-start(bf16[96,2,384]{2,1,0:T(2,128)(2,1)} %member_sum.1), calls=%async_computation.1 | async-start | bytes 294912 | tf_op jit(solution)/shard_map/all_to_all | solution.py:241
  51.6 1.0 %copy-start.1 = (bf16[1024,256]{1,0:T(8,128)(2,1)S(1)}, bf16[1024,256]{1,0:T(8,128)(2,1)}, u32[]{:S(2)}) copy-start(bf16[1024,256]{1,0:T(8,128)(2,1)} %get-tuple-element.16.dp_ref) | copy-start | bytes 1572868
  52.6 1.0 %copy-start.2 = (bf16[256,1024]{1,0:T(8,128)(2,1)S(1)}, bf16[256,1024]{1,0:T(8,128)(2,1)}, u32[]{:S(2)}) copy-start(bf16[256,1024]{1,0:T(8,128)(2,1)} %get-tuple-element.15.pushed_ref) | copy-start | bytes 1572868
  53.6 18.8 %copy-start.4 = (s32[1,96,2]{1,2,0:T(2,128)S(1)}, s32[1,96,2]{1,2,0:T(2,128)}, u32[]{:S(2)}) copy-start(s32[1,96,2]{1,2,0:T(2,128)} %param.25) | copy-start | bytes 2308
  66.5 18.8 %all-to-all-start.2 = ((bf16[96,2,128]{2,1,0:T(2,128)(2,1)}), bf16[96,2,128]{2,1,0:T(2,128)(2,1)S(1)}, u32[]{:S(2)}, u32[]{:S(2)}) async-start(bf16[96,2,128]{2,1,0:T(2,128)(2,1)} %grad_row.1), calls=%async_computation.2 | async-start | bytes 98304 | tf_op jit(solution)/shard_map/all_to_all | solution.py:249

commit v4 on v3

--- a/solution.py
+++ b/solution.py
@@ -18,10 +18,13 @@
     return lax.dot_general(first_op, second_op, (((1,), (1,)), ((), ())), preferred_element_type=F32)
 
 
-def identity(size):
-    row = lax.broadcasted_iota(jnp.int32, (size, size), 0)
-    col = lax.broadcasted_iota(jnp.int32, (size, size), 1)
-    return jnp.where(row == col, 1.0, 0.0).astype(BF16)
+def dot_tn(first_op, second_op):
+    return lax.dot_general(first_op, second_op, (((0,), (0,)), ((), ())), preferred_element_type=F32)
+
+
+def one_hot(index, count):
+    row = lax.broadcasted_iota(jnp.int16, (count, index.shape[1]), 0)
+    return jnp.where(row == index.astype(jnp.int16), jnp.ones((), BF16), jnp.zeros((), BF16))
 
 
 def edges_and_grads(groups, members, per_owner, scale, chunk):
@@ -49,7 +52,6 @@
         member = rest // per_owner
         which = rest - member * per_owner
         place = which * rows + member * groups + group
-        row = lax.broadcasted_iota(jnp.int32, (groups, edges), 0)
         pieces = [
             (ref, j, p, j * rows + (2 * p + parity) * groups)
             for ref, parity in ((send_ref, 1 - side), (keep_ref, side))
@@ -57,7 +59,7 @@
             for p in range(members // 2)
         ]
         for n, (_, _, _, first) in enumerate(pieces):
-            put_ref[n] = jnp.where(row == place - first, 1.0, 0.0).astype(BF16)
+            put_ref[n * groups : (n + 1) * groups, :] = one_hot(place - first, groups)
         for load in loads[3:6]:
             load.wait()
         x = preact_ref[...].astype(F32)
@@ -76,22 +78,21 @@
         all_terms = []
         for e0 in range(0, edges, chunk):
             dst = dst_ref[:, e0 : e0 + chunk]
-            node = lax.broadcasted_iota(jnp.int32, (nodes, chunk), 0)
-            take = jnp.where(node == dst, 1.0, 0.0).astype(BF16)
+            take = one_hot(dst, nodes)
             all_terms.append((dot_nn(pushed_t, take) * weight_ref[:, e0 : e0 + chunk]).astype(BF16))
         terms = jnp.concatenate(all_terms, axis=1)
 
+        sums = dot_nt(put_ref[...], terms).astype(BF16)
         for n, (ref, j, p, _) in enumerate(pieces):
-            ref[p, :, j * width : (j + 1) * width] = dot_nt(put_ref[n], terms).astype(BF16)
+            ref[p, :, j * width : (j + 1) * width] = sums[n * groups : (n + 1) * groups]
 
         for load in loads[6:]:
             load.wait()
-        eye = identity(width)
         share = 2 * width // members
         empty = jnp.zeros((groups - share, width), BF16)
         lanes = slice(per_owner * width, (per_owner + 1) * width)
         for i, ref in enumerate((feat_ref, agg_ref)):
-            grad = dot_nn(dot_nt(eye, ref[...]).astype(BF16), dp) * scale
+            grad = dot_tn(ref[...], dp) * scale
             for k in range(members // 4):
                 p = i * (members // 4) + k
                 low = grad[2 * k * share : (2 * k + 1) * share]
@@ -106,7 +107,15 @@
     return kernel
 
 
-def tiles_kernel(rows_ref, cols_ref, vals_ref, pushed_ref, dp_ref, ws_ref, out_ref, adj_ref):
+def tiles_kernel(
+    rows_ref, cols_ref, vals_ref, pushed_hbm, dp_hbm, ws_ref, out_ref, adj_ref, pushed_ref, dp_ref, in_sem
+):
+    loads = [
+        pltpu.make_async_copy(pushed_hbm, pushed_ref, in_sem.at[0]),
+        pltpu.make_async_copy(dp_hbm, dp_ref, in_sem.at[1]),
+    ]
+    for load in loads:
+        load.start()
     count, block, _ = vals_ref.shape
     adj_ref[...] = jnp.zeros_like(adj_ref)
 
@@ -117,6 +126,8 @@
         return carry
 
     lax.fori_loop(0, count, add, 0)
+    for load in loads:
+        load.wait()
     interior_t = dot_nn(pushed_ref[...], adj_ref[...].astype(BF16))
     out_ref[...] = dot_nt(dp_ref[...], ws_ref[...]) + interior_t.T
 
@@ -142,9 +153,7 @@
     arrived = jnp.concatenate([arrived_ref[:, 0, :], arrived_ref[:, 1, :]], axis=1)
     total = base_ref[...]
     for j in range(per_owner):
-        node = lax.broadcasted_iota(jnp.int32, (nodes, groups), 0)
-        put = jnp.where(node == target_ref[j : j + 1, :], 1.0, 0.0).astype(BF16)
-        total += dot_nn(put, arrived[:, j * width : (j + 1) * width])
+        total += dot_nn(one_hot(target_ref[j : j + 1, :], nodes), arrived[:, j * width : (j + 1) * width])
     out_ref[...] = total.astype(BF16)
 
 
@@ -210,7 +219,7 @@
         + [
             pltpu.VMEM((nodes, width), BF16),
             pltpu.VMEM((width, nodes), BF16),
-            pltpu.VMEM((members * per_owner, groups, edges), BF16),
+            pltpu.VMEM((members * per_owner * groups, edges), BF16),
             pltpu.SemaphoreType.DMA((len(operands),)),
             pltpu.SemaphoreType.DMA((2,)),
         ],
@@ -220,12 +229,24 @@
     base = pl.pallas_call(
         tiles_kernel,
         out_shape=jax.ShapeDtypeStruct((nodes, width), F32),
-        in_specs=[smem, smem, vmem, vmem, vmem, vmem],
+        in_specs=[smem, smem, vmem, hbm, hbm, vmem],
         out_specs=vmem,
-        scratch_shapes=[pltpu.VMEM((nodes, nodes), F32)],
+        scratch_shapes=[
+            pltpu.VMEM((nodes, nodes), F32),
+            pltpu.VMEM((width, nodes), BF16),
+            pltpu.VMEM((nodes, width), BF16),
+            pltpu.SemaphoreType.DMA((2,)),
+        ],
         compiler_params=params,
         name="tiles",
-    )(tile_rows, tile_cols, tile_vals, pushed_t, dp, w_self)
+    )(
+        tile_rows,
+        tile_cols,
+        tile_vals,
+        pltpu.with_memory_space_constraint(pushed_t, pltpu.HBM),
+        pltpu.with_memory_space_constraint(dp, pltpu.HBM),
+        w_self,
+    )
 
     other_core = [(i, i ^ 1) for i in range(members)]
     along_x = [list(range(core, members, 2)) for core in range(2)]

time: 101 us -> 96.7 us (0.957)
  Pallas kernels: 16.6 us -> 12.8 us
  waiting for transfers between devices: 22.4 us -> 24.5 us
  local copies, waits for them, and re-layouts: 2.27 us -> 0.19 us
    pallas_call x1, Pallas kernels: 9.47 us -> 5.65 us  [on_device(): pl.pallas_call(edges_and_grads(groups, members, per_owner, scale, 512), o...]
    unnamed x14 -> x10, local copies, waits for them, and re-layouts: 2.1 us -> 0.03 us
    all_to_all x1, waiting for transfers between devices: 9.4 us -> 11.5 us  [on_device(): arrived = lax.all_to_all(summed, 'group', 0, 0, tiled=True)]
where the time goes in v4:
time: 96.7 us; the launch traced here: 96.3 us
  starting transfers between devices  32.4 us (34%)
  blocking collectives  25.5 us (26%)
  waiting for transfers between devices  24.5 us (25%)
  Pallas kernels  12.8 us (13%)
    all_to_all x1, starting transfers between devices, on_device(): arrived = lax.all_to_all(summed, 'group', 0, 0, tiled=True)  14.1 us
    all_to_all x1, blocking collectives, on_device(): grads = lax.all_to_all(mine, 'local', 0, 0, tiled=True)  13.4 us
    ppermute x1, starting transfers between devices, on_device(): came = lax.ppermute(send, 'local', other_core)  12.4 us
    all_to_all x1, blocking collectives, on_device(): lax.all_to_all(chip_sum, 'local', 0, 0, axis_index_groups=along_x, tiled=...  12.2 us
    all_to_all x1, waiting for transfers between devices, on_device(): arrived = lax.all_to_all(summed, 'group', 0, 0, tiled=True)  11.5 us
    all_to_all x1, waiting for transfers between devices, on_device(): spread = lax.all_to_all(rows, 'group', 0, 0, tiled=True)  11.4 us
    all_to_all x1, starting transfers between devices, on_device(): spread = lax.all_to_all(rows, 'group', 0, 0, tiled=True)  5.92 us
    pallas_call x1, Pallas kernels, on_device(): pl.pallas_call(edges_and_grads(groups, members, per_owner, scale, 512), o...  5.65 us
  transfers between devices with their start and end apart: 3, of which 3 were waited for; matrix products, arithmetic and copies ran while one was open for 0% of the time, Pallas kernels for 4%

profile of v4, /device:TPU:1, one launch (start us, length us, event | category | flops | bytes accessed | tf_op | source)
XLA Modules:
  0.0 96.3 jit_solution(10371279427964521092)
XLA Ops:
  0.6 5.6 %edges_and_grads.1 = (bf16[1024,256]{1,0:T(8,128)(2,1)}, bf16[256,1024]{1,0:T(8,128)(2,1)}, bf16[4,96,768]{2,1,0:T(8,128)(2,1)S(1)}, bf16[4,96,768]{2,1,0:T(8,128)(2,1)S(1)}) custom-call(s32[1,2048]{1,0:T(1,128)} %bitcast.7, s32[1,2048]{1,0:T(1,128)} %bitcast.8, f32[1,2048]{1,0:T(1,128)} %bitcast.9, bf16[1024,256]{1,0:T(8,128)(2,1)} %preact_hbm.1, ...), custom_call_target="tpu_custom_call" | custom-call | tf_op jit(solution)/shard_map/edges_and_grads/pallas_call | solution.py:208
  6.3 12.4 %collective-permute-start = (bf16[4,96,768]{2,1,0:T(8,128)(2,1)S(1)}, bf16[4,96,768]{2,1,0:T(8,128)(2,1)S(1)}, u32[]{:S(2)}, u32[]{:S(2)}) collective-permute-start(bf16[4,96,768]{2,1,0:T(8,128)(2,1)S(1)} %get-tuple-element.13), channel_id=1, source_target_pairs={{0,1},{1,0},{2,3},{3,2},{4,5},{5,4},{6,7},{7,6},{8,9},{9,8},{10,11... | collective-permute-start | bytes 1769480 | tf_op jit(solution)/shard_map/ppermute | solution.py:253
  18.7 1.6 %collective-permute-done = bf16[4,96,768]{2,1,0:T(8,128)(2,1)S(1)} collective-permute-done((bf16[4,96,768]{2,1,0:T(8,128)(2,1)S(1)}, bf16[4,96,768]{2,1,0:T(8,128)(2,1)S(1)}, u32[]{:S(2)}, u32[]{:S(2)}) %collective-permute-start) | collective-permute-done | bytes 589856 | tf_op jit(solution)/shard_map/ppermute | solution.py:253
  20.3 0.0 copy-start.1
  20.3 0.1 add_convert_fusion
  20.5 0.0 copy-start
  20.5 0.0 copy-start.3
  20.5 0.0 copy-start.4
  20.5 12.2 %all_to_all.20.parts_ref = bf16[4,96,768]{2,1,0:T(8,128)(2,1)S(1)} all-to-all(bf16[4,96,768]{2,1,0:T(8,128)(2,1)S(1)} %add_convert_fusion), channel_id=1, replica_groups={{0,2,4,6},{1,3,5,7},{8,10,12,14},{9,11,13,15},{16,18,20,22},{17,19,21,2..., dimensions={0} | all-to-all | bytes 1179648 | tf_op jit(solution)/shard_map/all_to_all | solution.py:255
  32.7 0.9 member_sum.1
  33.6 14.1 %all-to-all-start.1 = ((bf16[96,2,384]{2,1,0:T(2,128)(2,1)}), bf16[96,2,384]{2,1,0:T(2,128)(2,1)S(1)}, u32[]{:S(2)}, u32[]{:S(2)}) async-start(bf16[96,2,384]{2,1,0:T(2,128)(2,1)} %member_sum.1), calls=%async_computation.1 | async-start | bytes 294912 | tf_op jit(solution)/shard_map/all_to_all | solution.py:262
  47.7 0.0 copy-done.1
  47.7 0.0 copy-done
  47.7 0.0 copy-done.3
  47.7 0.0 copy-done.4
  47.7 0.0 copy-start.2
  47.7 2.7 %tiles.1.base_ref = f32[1024,256]{1,0:T(8,128)S(1)} custom-call(s32[64]{0:T(128)S(1)} %copy-done.3, s32[64]{0:T(128)S(1)} %copy-done.4, bf16[64,128,128]{2,1,0:T(8,128)(2,1)S(1)} %copy-done, bf16[256,1024]{1,0:T(8,128)(2,1)} %get-tuple-element.15.pushed_hbm, bf16[1024,256]{1,0:T(8,128)(2,1)} %get-tuple-element.16.dp_hbm, bf16[256,256]{1,0:T(8,128)(2,1)S(1)} %copy-done.1), custom_call_target="tpu_custom_call" | custom-call | tf_op jit(solution)/shard_map/tiles/pallas_call | solution.py:229
  50.5 11.5 %all-to-all-done.1.arrived_ref = bf16[96,2,384]{2,1,0:T(2,128)(2,1)S(1)} async-done(((bf16[96,2,384]{2,1,0:T(2,128)(2,1)}), bf16[96,2,384]{2,1,0:T(2,128)(2,1)S(1)}, u32[]{:S(2)}, u32[]{:S(2)}) %all-to-all-start.1) | async-done | bytes 147488 | tf_op jit(solution)/shard_map/all_to_all | solution.py:262
  61.9 0.8 grad_row.1
  62.7 5.9 %all-to-all-start.2 = ((bf16[96,2,128]{2,1,0:T(2,128)(2,1)}), bf16[96,2,128]{2,1,0:T(2,128)(2,1)S(1)}, u32[]{:S(2)}, u32[]{:S(2)}) async-start(bf16[96,2,128]{2,1,0:T(2,128)(2,1)} %grad_row.1), calls=%async_computation.2 | async-start | bytes 98304 | tf_op jit(solution)/shard_map/all_to_all | solution.py:270
  68.6 0.0 copy-done.2
  68.6 1.5 %finish.1 = bf16[1024,256]{1,0:T(8,128)(2,1)} custom-call(bf16[96,2,384]{2,1,0:T(2,128)(2,1)S(1)} %all-to-all-done.1.arrived_ref, s32[2,96]{1,0:T(2,128)S(1)} %bitcast.6, f32[1024,256]{1,0:T(8,128)S(1)} %tiles.1.base_ref), custom_call_target="tpu_custom_call" | custom-call | tf_op jit(solution)/shard_map/finish/pallas_call | solution.py:271
  70.1 11.4 %all-to-all-done.2 = bf16[96,2,128]{2,1,0:T(2,128)(2,1)S(1)} async-done(((bf16[96,2,128]{2,1,0:T(2,128)(2,1)}), bf16[96,2,128]{2,1,0:T(2,128)(2,1)S(1)}, u32[]{:S(2)}, u32[]{:S(2)}) %all-to-all-start.2) | async-done | bytes 49184 | tf_op jit(solution)/shard_map/all_to_all | solution.py:270
  81.6 0.1 broadcast_in_dim.2
  81.7 13.4 %all_to_all.21.grads_ref = bf16[8,64,2,128]{3,2,1,0:T(2,128)(2,1)S(1)} all-to-all(bf16[8,64,2,128]{3,2,1,0:T(2,128)(2,1)S(1)} %broadcast_in_dim.2), channel_id=1, replica_groups=mesh['group'=96,'local'=8] {'local'}, dimensions={0} | all-to-all | bytes 524288 | tf_op jit(solution)/shard_map/all_to_all | solution.py:279
  95.1 1.2 %widen.1 = (f32[256,256]{1,0:T(8,128)}, f32[256,256]{1,0:T(8,128)}) custom-call(bf16[8,64,2,128]{3,2,1,0:T(2,128)(2,1)S(1)} %all_to_all.21.grads_ref), custom_call_target="tpu_custom_call" | custom-call | tf_op jit(solution)/shard_map/widen/pallas_call | solution.py:280
  (1 shorter events, 0.0 us)
Async XLA Ops:
  6.3 14.0 %collective-permute-start = (bf16[4,96,768]{2,1,0:T(8,128)(2,1)S(1)}, bf16[4,96,768]{2,1,0:T(8,128)(2,1)S(1)}, u32[]{:S(2)}, u32[]{:S(2)}) collective-permute-start(bf16[4,96,768]{2,1,0:T(8,128)(2,1)S(1)} %get-tuple-element.13), channel_id=1, source_target_pairs={{0,1},{1,0},{2,3},{3,2},{4,5},{5,4},{6,7},{7,6},{8,9},{9,8},{10,11... | collective-permute-start | bytes 1769480 | tf_op jit(solution)/shard_map/ppermute | solution.py:253
  20.3 27.4 %copy-start.1 = (bf16[256,256]{1,0:T(8,128)(2,1)S(1)}, bf16[256,256]{1,0:T(8,128)(2,1)}, u32[]{:S(2)}) copy-start(bf16[256,256]{1,0:T(8,128)(2,1)} %ws_ref.1) | copy-start | bytes 393220
  20.5 27.2 %copy-start = (bf16[64,128,128]{2,1,0:T(8,128)(2,1)S(1)}, bf16[64,128,128]{2,1,0:T(8,128)(2,1)}, u32[]{:S(2)}) copy-start(bf16[64,128,128]{2,1,0:T(8,128)(2,1)} %vals_ref.1) | copy-start | bytes 6291460
  20.5 27.2 %copy-start.3 = (s32[64]{0:T(128)S(1)}, s32[64]{0:T(128)}, u32[]{:S(2)}) copy-start(s32[64]{0:T(128)} %rows_ref.1) | copy-start | bytes 772
  20.5 27.2 %copy-start.4 = (s32[64]{0:T(128)S(1)}, s32[64]{0:T(128)}, u32[]{:S(2)}) copy-start(s32[64]{0:T(128)} %cols_ref.1) | copy-start | bytes 772
  33.6 28.4 %all-to-all-start.1 = ((bf16[96,2,384]{2,1,0:T(2,128)(2,1)}), bf16[96,2,384]{2,1,0:T(2,128)(2,1)S(1)}, u32[]{:S(2)}, u32[]{:S(2)}) async-start(bf16[96,2,384]{2,1,0:T(2,128)(2,1)} %member_sum.1), calls=%async_computation.1 | async-start | bytes 294912 | tf_op jit(solution)/shard_map/all_to_all | solution.py:262
  47.7 20.9 %copy-start.2 = (s32[1,96,2]{1,2,0:T(2,128)S(1)}, s32[1,96,2]{1,2,0:T(2,128)}, u32[]{:S(2)}) copy-start(s32[1,96,2]{1,2,0:T(2,128)} %param.25) | copy-start | bytes 2308
  62.7 18.8 %all-to-all-start.2 = ((bf16[96,2,128]{2,1,0:T(2,128)(2,1)}), bf16[96,2,128]{2,1,0:T(2,128)(2,1)S(1)}, u32[]{:S(2)}, u32[]{:S(2)}) async-start(bf16[96,2,128]{2,1,0:T(2,128)(2,1)} %grad_row.1), calls=%async_computation.2 | async-start | bytes 98304 | tf_op jit(solution)/shard_map/all_to_all | solution.py:270

commit v5 on v4

--- a/solution.py
+++ b/solution.py
@@ -8,6 +8,7 @@
 F32 = jnp.float32
 BF16 = jnp.bfloat16
 VMEM_LIMIT = 24 * 1024 * 1024
+OWNERS = 16
 
 
 def dot_nn(first_op, second_op):
@@ -84,23 +85,20 @@
 
         sums = dot_nt(put_ref[...], terms).astype(BF16)
         for n, (ref, j, p, _) in enumerate(pieces):
-            ref[p, :, j * width : (j + 1) * width] = sums[n * groups : (n + 1) * groups]
+            ref[p, j * groups : (j + 1) * groups] = sums[n * groups : (n + 1) * groups]
 
         for load in loads[6:]:
             load.wait()
         share = 2 * width // members
-        empty = jnp.zeros((groups - share, width), BF16)
-        lanes = slice(per_owner * width, (per_owner + 1) * width)
+        tail = slice(per_owner * groups, per_owner * groups + share)
         for i, ref in enumerate((feat_ref, agg_ref)):
             grad = dot_tn(ref[...], dp) * scale
             for k in range(members // 4):
                 p = i * (members // 4) + k
                 low = grad[2 * k * share : (2 * k + 1) * share]
                 high = grad[(2 * k + 1) * share : (2 * k + 2) * share]
-                send_ref[p, 0:share, lanes] = jnp.where(side == 0, high, low).astype(BF16)
-                keep_ref[p, 0:share, lanes] = jnp.where(side == 0, low, high).astype(BF16)
-                send_ref[p, share:, lanes] = empty
-                keep_ref[p, share:, lanes] = empty
+                send_ref[p, tail] = jnp.where(side == 0, high, low).astype(BF16)
+                keep_ref[p, tail] = jnp.where(side == 0, low, high).astype(BF16)
         for store in stores:
             store.wait()
 
@@ -132,38 +130,57 @@
     out_ref[...] = dot_nt(dp_ref[...], ws_ref[...]) + interior_t.T
 
 
-def member_sum_kernel(parts_ref, out_ref):
-    total = jnp.sum(parts_ref[...].astype(F32), axis=0)
-    half = out_ref.shape[2]
-    out_ref[:, 0, :] = total[:, :half].astype(BF16)
-    out_ref[:, 1, :] = total[:, half:].astype(BF16)
-
-
-def grad_row_kernel(arrived_ref, out_ref):
-    half = out_ref.shape[2]
-    row = jnp.sum(arrived_ref[:, 1, half:].astype(F32), axis=0, keepdims=True).astype(BF16)
-    for k in range(2):
-        out_ref[:, k, :] = jnp.broadcast_to(row[:, k * half : (k + 1) * half], (out_ref.shape[0], half))
+def member_sum(per_owner, owners):
+    def kernel(parts_ref, out_ref):
+        total = jnp.sum(parts_ref[...].astype(F32), axis=0).astype(BF16)
+        groups = out_ref.shape[0]
+        width = total.shape[1]
+        pieces = [total[j * groups : (j + 1) * groups] for j in range(per_owner)]
+        for first in range(per_owner * groups, total.shape[0], owners):
+            pieces.append(jnp.concatenate([total[first : first + owners]] * (groups // owners), axis=0))
+        per_line = len(pieces) // 2
+        for n, piece in enumerate(pieces):
+            k, at = n // per_line, n % per_line * width
+            out_ref[:, k, at : at + width] = piece
+
+    return kernel
+
+
+def grad_rows(per_owner, width):
+    def kernel(arrived_ref, out_ref):
+        per_line = arrived_ref.shape[2] // width
+        owners, lines, lanes = out_ref.shape
+        rows = []
+        for n in range(per_owner, 2 * per_line):
+            k, at = n // per_line, n % per_line * width
+            row = jnp.sum(arrived_ref[:, k, at : at + width].astype(F32), axis=0, keepdims=True)
+            rows += [row[:, h : h + lanes] for h in range(0, width, lanes)]
+        tile = jnp.concatenate(rows, axis=0)
+        out_ref[...] = jnp.broadcast_to(tile[None], (owners, lines, lanes)).astype(BF16)
+
+    return kernel
 
 
 def finish_kernel(arrived_ref, target_ref, base_ref, out_ref):
     nodes, width = out_ref.shape
-    groups = arrived_ref.shape[0]
-    per_owner = target_ref.shape[0]
-    arrived = jnp.concatenate([arrived_ref[:, 0, :], arrived_ref[:, 1, :]], axis=1)
     total = base_ref[...]
-    for j in range(per_owner):
-        total += dot_nn(one_hot(target_ref[j : j + 1, :], nodes), arrived[:, j * width : (j + 1) * width])
+    for j in range(target_ref.shape[0]):
+        put = one_hot(target_ref[j : j + 1, :], nodes)
+        total += dot_nn(put, arrived_ref[:, 0, j * width : (j + 1) * width])
     out_ref[...] = total.astype(BF16)
 
 
 def widen_kernel(grads_ref, self_ref, neigh_ref):
-    members, share, _, half = grads_ref.shape
+    members, owners, lines, lanes = grads_ref.shape
+    per_row = self_ref.shape[1] // lanes
+    share = owners * lines // per_row
     for m in range(members):
         ref = (self_ref, neigh_ref)[2 * m // members]
         first = m % (members // 2) * share
-        for k in range(2):
-            ref[first : first + share, k * half : (k + 1) * half] = grads_ref[m, :, k, :].astype(F32)
+        part = grads_ref[m].astype(F32)
+        for n in range(lines):
+            at, col = first + n // per_row * owners, n % per_row * lanes
+            ref[at : at + owners, col : col + lanes] = part[:, n, :]
 
 
 def on_device(
@@ -187,8 +204,10 @@
     edges = edge_dst.shape[0]
     per_owner = recv_rows.shape[2]
     scale = (nodes * groups * members) ** (-0.5)
-    payload = (per_owner + 1) * width
     share = 2 * width // members
+    rows_held = share // OWNERS
+    payload = (per_owner + rows_held) * width
+    lines = rows_held * width // 128
     params = pltpu.CompilerParams(vmem_limit_bytes=VMEM_LIMIT)
     smem = pl.BlockSpec(memory_space=pltpu.SMEM)
     vmem = pl.BlockSpec(memory_space=pltpu.VMEM)
@@ -204,7 +223,7 @@
         features,
         aggregate,
     )
-    half = jax.ShapeDtypeStruct((members // 2, groups, payload), BF16)
+    half = jax.ShapeDtypeStruct((members // 2, per_owner * groups + share, width), BF16)
     dp, pushed_t, send, keep = pl.pallas_call(
         edges_and_grads(groups, members, per_owner, scale, 512),
         out_shape=(
@@ -254,20 +273,21 @@
     chip_sum = (came.astype(F32) + keep.astype(F32)).astype(BF16)
     parts = lax.all_to_all(chip_sum, "local", 0, 0, axis_index_groups=along_x, tiled=True)
     summed = pl.pallas_call(
-        member_sum_kernel,
+        member_sum(per_owner, OWNERS),
         out_shape=jax.ShapeDtypeStruct((groups, 2, payload // 2), BF16),
         compiler_params=params,
         name="member_sum",
     )(parts)
     arrived = lax.all_to_all(summed, "group", 0, 0, tiled=True)
     rows = pl.pallas_call(
-        grad_row_kernel,
-        out_shape=jax.ShapeDtypeStruct((groups, 2, width // 2), BF16),
-        compiler_params=params,
-        name="grad_row",
+        grad_rows(per_owner, width),
+        out_shape=jax.ShapeDtypeStruct((OWNERS, lines, 128), BF16),
+        compiler_params=params,
+        name="grad_rows",
     )(arrived)
     rows, base = lax.optimization_barrier((rows, base))
-    spread = lax.all_to_all(rows, "group", 0, 0, tiled=True)
+    blocks = [list(range(first, first + OWNERS)) for first in range(0, groups, OWNERS)]
+    spread = lax.all_to_all(rows, "group", 0, 0, axis_index_groups=blocks, tiled=True)
     grad_x = pl.pallas_call(
         finish_kernel,
         out_shape=jax.ShapeDtypeStruct((nodes, width), BF16),
@@ -275,7 +295,7 @@
         name="finish",
     )(arrived, recv_rows.reshape(groups, per_owner).T, base)
     spread, grad_x = lax.optimization_barrier((spread, grad_x))
-    mine = jnp.broadcast_to(spread[None, :share], (members, share, 2, width // 2))
+    mine = jnp.broadcast_to(spread[None], (members, OWNERS, lines, 128))
     grads = lax.all_to_all(mine, "local", 0, 0, tiled=True)
     grad_self, grad_neigh = pl.pallas_call(
         widen_kernel,

time: 96.7 us -> 91.7 us (0.948)
  waiting for transfers between devices: 24.5 us -> 21.5 us
  starting transfers between devices: 32.4 us -> 29.6 us
    all_to_all x1, waiting for transfers between devices: 11.4 us -> 5.87 us  [on_device(): lax.all_to_all(rows, 'group', 0, 0, axis_index_groups=blocks, tiled=True)]
    all_to_all x1, waiting for transfers between devices: 11.5 us -> 14.1 us  [on_device(): arrived = lax.all_to_all(summed, 'group', 0, 0, tiled=True)]
    all_to_all x1, starting transfers between devices: 5.92 us -> 3.5 us  [on_device(): lax.all_to_all(rows, 'group', 0, 0, axis_index_groups=blocks, tiled=True)]
  transfers between devices with their start and end apart: 3 -> 3, of which waited for: 3 -> 3; matrix products, arithmetic and copies ran while one was open for 0% -> 0% of each run, Pallas kernels for 4% -> 5%
where the time goes in v5:
time: 91.7 us; the launch traced here: 91.3 us
  starting transfers between devices  29.6 us (32%)
  blocking collectives  25.7 us (28%)
  waiting for transfers between devices  21.5 us (23%)
  Pallas kernels  12.7 us (14%)
  local copies, waits for them, and re-layouts  0.96 us (1%)
    all_to_all x1, waiting for transfers between devices, on_device(): arrived = lax.all_to_all(summed, 'group', 0, 0, tiled=True)  14.1 us
    all_to_all x1, blocking collectives, on_device(): grads = lax.all_to_all(mine, 'local', 0, 0, tiled=True)  14 us
    all_to_all x1, starting transfers between devices, on_device(): arrived = lax.all_to_all(summed, 'group', 0, 0, tiled=True)  13.5 us
    ppermute x1, starting transfers between devices, on_device(): came = lax.ppermute(send, 'local', other_core)  12.6 us
    all_to_all x1, blocking collectives, on_device(): lax.all_to_all(chip_sum, 'local', 0, 0, axis_index_groups=along_x, tiled=...  11.6 us
    all_to_all x1, waiting for transfers between devices, on_device(): lax.all_to_all(rows, 'group', 0, 0, axis_index_groups=blocks, tiled=True)  5.87 us
    pallas_call x1, Pallas kernels, on_device(): pl.pallas_call(edges_and_grads(groups, members, per_owner, scale, 512), o...  5.65 us
    all_to_all x1, starting transfers between devices, on_device(): lax.all_to_all(rows, 'group', 0, 0, axis_index_groups=blocks, tiled=True)  3.5 us
  transfers between devices with their start and end apart: 3, of which 3 were waited for; matrix products, arithmetic and copies ran while one was open for 0% of the time, Pallas kernels for 5%

profile of v5, /device:TPU:1, one launch (start us, length us, event | category | flops | bytes accessed | tf_op | source)
XLA Modules:
  0.0 91.3 jit_solution(2051674349658924608)
XLA Ops:
  0.6 5.6 %edges_and_grads.1 = (bf16[1024,256]{1,0:T(8,128)(2,1)}, bf16[256,1024]{1,0:T(8,128)(2,1)}, bf16[4,256,256]{2,1,0:T(8,128)(2,1)S(1)}, bf16[4,256,256]{2,1,0:T(8,128)(2,1)S(1)}) custom-call(s32[1,2048]{1,0:T(1,128)} %bitcast.7, s32[1,2048]{1,0:T(1,128)} %bitcast.8, f32[1,2048]{1,0:T(1,128)} %bitcast.9, bf16[1024,256]{1,0:T(8,128)(2,1)} %preact_hbm.1, ...), custom_call_target="tpu_custom_call" | custom-call | tf_op jit(solution)/shard_map/edges_and_grads/pallas_call | solution.py:227
  6.3 0.0 copy-start
  6.3 0.0 copy-start.3
  6.3 0.0 copy-start.4
  6.3 12.6 %collective-permute-start = (bf16[4,256,256]{2,1,0:T(8,128)(2,1)S(1)}, bf16[4,256,256]{2,1,0:T(8,128)(2,1)S(1)}, u32[]{:S(2)}, u32[]{:S(2)}) collective-permute-start(bf16[4,256,256]{2,1,0:T(8,128)(2,1)S(1)} %get-tuple-element.13), channel_id=1, source_target_pairs={{0,1},{1,0},{2,3},{3,2},{4,5},{5,4},{6,7},{7,6},{8,9},{9,8},{10,11... | collective-permute-start | bytes 1572872 | tf_op jit(solution)/shard_map/ppermute | solution.py:272
  18.9 1.5 %collective-permute-done = bf16[4,256,256]{2,1,0:T(8,128)(2,1)S(1)} collective-permute-done((bf16[4,256,256]{2,1,0:T(8,128)(2,1)S(1)}, bf16[4,256,256]{2,1,0:T(8,128)(2,1)S(1)}, u32[]{:S(2)}, u32[]{:S(2)}) %collective-permute-start) | collective-permute-done | bytes 524320 | tf_op jit(solution)/shard_map/ppermute | solution.py:272
  20.4 0.1 add_convert_fusion
  20.5 11.6 %all_to_all.20.parts_ref = bf16[4,256,256]{2,1,0:T(8,128)(2,1)S(1)} all-to-all(bf16[4,256,256]{2,1,0:T(8,128)(2,1)S(1)} %add_convert_fusion), channel_id=1, replica_groups={{0,2,4,6},{1,3,5,7},{8,10,12,14},{9,11,13,15},{16,18,20,22},{17,19,21,2..., dimensions={0} | all-to-all | bytes 1048576 | tf_op jit(solution)/shard_map/all_to_all | solution.py:274
  32.2 1.1 %member_sum.1 = bf16[96,2,768]{2,1,0:T(2,128)(2,1)} custom-call(bf16[4,256,256]{2,1,0:T(8,128)(2,1)S(1)} %all_to_all.20.parts_ref), custom_call_target="tpu_custom_call" | custom-call | tf_op jit(solution)/shard_map/member_sum/pallas_call | solution.py:275
  33.2 13.5 %all-to-all-start.1 = ((bf16[96,2,768]{2,1,0:T(2,128)(2,1)}), bf16[96,2,768]{2,1,0:T(2,128)(2,1)S(1)}, u32[]{:S(2)}, u32[]{:S(2)}) async-start(bf16[96,2,768]{2,1,0:T(2,128)(2,1)} %member_sum.1), calls=%async_computation.1 | async-start | bytes 589824 | tf_op jit(solution)/shard_map/all_to_all | solution.py:281
  46.8 0.0 copy-done
  46.8 0.0 copy-done.3
  46.8 0.0 copy-done.4
  46.8 0.0 copy-start.1
  46.8 0.9 copy-done.1
  47.7 0.0 copy-start.2
  47.7 2.7 %tiles.1.base_ref = f32[1024,256]{1,0:T(8,128)S(1)} custom-call(s32[64]{0:T(128)S(1)} %copy-done.3, s32[64]{0:T(128)S(1)} %copy-done.4, bf16[64,128,128]{2,1,0:T(8,128)(2,1)S(1)} %copy-done, bf16[256,1024]{1,0:T(8,128)(2,1)} %get-tuple-element.15.pushed_hbm, bf16[1024,256]{1,0:T(8,128)(2,1)} %get-tuple-element.16.dp_hbm, bf16[256,256]{1,0:T(8,128)(2,1)S(1)} %copy-done.1), custom_call_target="tpu_custom_call" | custom-call | tf_op jit(solution)/shard_map/tiles/pallas_call | solution.py:248
  50.4 14.1 %all-to-all-done.1.arrived_ref = bf16[96,2,768]{2,1,0:T(2,128)(2,1)S(1)} async-done(((bf16[96,2,768]{2,1,0:T(2,128)(2,1)}), bf16[96,2,768]{2,1,0:T(2,128)(2,1)S(1)}, u32[]{:S(2)}, u32[]{:S(2)}) %all-to-all-start.1) | async-done | bytes 294944 | tf_op jit(solution)/shard_map/all_to_all | solution.py:281
  64.5 0.9 grad_rows.1
  65.4 3.5 %all-to-all-start.2 = ((bf16[16,8,128]{2,1,0:T(8,128)(2,1)}), bf16[16,8,128]{2,1,0:T(8,128)(2,1)S(1)}, u32[]{:S(2)}, u32[]{:S(2)}) async-start(bf16[16,8,128]{2,1,0:T(8,128)(2,1)} %grad_rows.1), calls=%async_computation.2 | async-start | bytes 65536 | tf_op jit(solution)/shard_map/all_to_all | solution.py:290
  68.9 0.0 copy-done.2
  68.9 1.4 %finish.1 = bf16[1024,256]{1,0:T(8,128)(2,1)} custom-call(bf16[96,2,768]{2,1,0:T(2,128)(2,1)S(1)} %all-to-all-done.1.arrived_ref, s32[2,96]{1,0:T(2,128)S(1)} %bitcast.6, f32[1024,256]{1,0:T(8,128)S(1)} %tiles.1.base_ref), custom_call_target="tpu_custom_call" | custom-call | tf_op jit(solution)/shard_map/finish/pallas_call | solution.py:291
  70.4 5.9 %all-to-all-done.2 = bf16[16,8,128]{2,1,0:T(8,128)(2,1)S(1)} async-done(((bf16[16,8,128]{2,1,0:T(8,128)(2,1)}), bf16[16,8,128]{2,1,0:T(8,128)(2,1)S(1)}, u32[]{:S(2)}, u32[]{:S(2)}) %all-to-all-start.2) | async-done | bytes 32800 | tf_op jit(solution)/shard_map/all_to_all | solution.py:290
  76.3 14.0 %all_to_all.21.grads_ref = bf16[8,16,8,128]{3,2,1,0:T(8,128)(2,1)S(1)} all-to-all(bf16[8,16,8,128]{3,2,1,0:T(8,128)(2,1)S(1)} %broadcast_in_dim.2), channel_id=1, replica_groups=mesh['group'=96,'local'=8] {'local'}, dimensions={0} | all-to-all | bytes 524288 | tf_op jit(solution)/shard_map/all_to_all | solution.py:299
  90.3 1.0 %widen.1 = (f32[256,256]{1,0:T(8,128)}, f32[256,256]{1,0:T(8,128)}) custom-call(bf16[8,16,8,128]{3,2,1,0:T(8,128)(2,1)S(1)} %all_to_all.21.grads_ref), custom_call_target="tpu_custom_call" | custom-call | tf_op jit(solution)/shard_map/widen/pallas_call | solution.py:300
  (1 shorter events, 0.0 us)
Async XLA Ops:
  6.3 40.5 %copy-start = (bf16[64,128,128]{2,1,0:T(8,128)(2,1)S(1)}, bf16[64,128,128]{2,1,0:T(8,128)(2,1)}, u32[]{:S(2)}) copy-start(bf16[64,128,128]{2,1,0:T(8,128)(2,1)} %vals_ref.1) | copy-start | bytes 6291460
  6.3 40.5 %copy-start.3 = (s32[64]{0:T(128)S(1)}, s32[64]{0:T(128)}, u32[]{:S(2)}) copy-start(s32[64]{0:T(128)} %rows_ref.1) | copy-start | bytes 772
  6.3 40.5 %copy-start.4 = (s32[64]{0:T(128)S(1)}, s32[64]{0:T(128)}, u32[]{:S(2)}) copy-start(s32[64]{0:T(128)} %cols_ref.1) | copy-start | bytes 772
  6.3 14.1 %collective-permute-start = (bf16[4,256,256]{2,1,0:T(8,128)(2,1)S(1)}, bf16[4,256,256]{2,1,0:T(8,128)(2,1)S(1)}, u32[]{:S(2)}, u32[]{:S(2)}) collective-permute-start(bf16[4,256,256]{2,1,0:T(8,128)(2,1)S(1)} %get-tuple-element.13), channel_id=1, source_target_pairs={{0,1},{1,0},{2,3},{3,2},{4,5},{5,4},{6,7},{7,6},{8,9},{9,8},{10,11... | collective-permute-start | bytes 1572872 | tf_op jit(solution)/shard_map/ppermute | solution.py:272
  33.2 31.3 %all-to-all-start.1 = ((bf16[96,2,768]{2,1,0:T(2,128)(2,1)}), bf16[96,2,768]{2,1,0:T(2,128)(2,1)S(1)}, u32[]{:S(2)}, u32[]{:S(2)}) async-start(bf16[96,2,768]{2,1,0:T(2,128)(2,1)} %member_sum.1), calls=%async_computation.1 | async-start | bytes 589824 | tf_op jit(solution)/shard_map/all_to_all | solution.py:281
  46.8 0.9 copy-start.1
  47.7 21.2 %copy-start.2 = (s32[1,96,2]{1,2,0:T(2,128)S(1)}, s32[1,96,2]{1,2,0:T(2,128)}, u32[]{:S(2)}) copy-start(s32[1,96,2]{1,2,0:T(2,128)} %param.25) | copy-start | bytes 2308
  65.4 10.8 %all-to-all-start.2 = ((bf16[16,8,128]{2,1,0:T(8,128)(2,1)}), bf16[16,8,128]{2,1,0:T(8,128)(2,1)S(1)}, u32[]{:S(2)}, u32[]{:S(2)}) async-start(bf16[16,8,128]{2,1,0:T(8,128)(2,1)} %grad_rows.1), calls=%async_computation.2 | async-start | bytes 65536 | tf_op jit(solution)/shard_map/all_to_all | solution.py:290

commit v6 on v5

--- a/solution.py
+++ b/solution.py
@@ -28,10 +28,26 @@
     return jnp.where(row == index.astype(jnp.int16), jnp.ones((), BF16), jnp.zeros((), BF16))
 
 
+def fill_slots(put_ref, place, parity, groups, members, per_owner):
+    for j in range(per_owner):
+        for p in range(members // 2):
+            first = j * members * groups + (2 * p + parity) * groups
+            at = (j * (members // 2) + p) * groups
+            put_ref[at : at + groups, :] = one_hot(place - first, groups)
+
+
+def store_slots(ref, sums, groups, per_owner):
+    sums = sums.astype(BF16)
+    for j in range(per_owner):
+        for p in range(ref.shape[0]):
+            at = (j * ref.shape[0] + p) * groups
+            ref[p, j * groups : (j + 1) * groups] = sums[at : at + groups]
+
+
 def edges_and_grads(groups, members, per_owner, scale, chunk):
     def kernel(
         dst_hbm, slot_hbm, weight_hbm, preact_hbm, cot_hbm, wn_hbm, feat_hbm, agg_hbm,
-        dp_hbm, pushed_hbm, send_ref, keep_ref,
+        dp_hbm, pushed_hbm, send_ref, tail_ref, terms_ref, place_ref,
         dst_ref, slot_ref, weight_ref, preact_ref, cot_ref, wn_ref, feat_ref, agg_ref,
         dp_ref, pushed_ref, put_ref, in_sem, out_sem,
     ):
@@ -53,14 +69,8 @@
         member = rest // per_owner
         which = rest - member * per_owner
         place = which * rows + member * groups + group
-        pieces = [
-            (ref, j, p, j * rows + (2 * p + parity) * groups)
-            for ref, parity in ((send_ref, 1 - side), (keep_ref, side))
-            for j in range(per_owner)
-            for p in range(members // 2)
-        ]
-        for n, (_, _, _, first) in enumerate(pieces):
-            put_ref[n * groups : (n + 1) * groups, :] = one_hot(place - first, groups)
+        place_ref[...] = place
+        fill_slots(put_ref, place, 1 - side, groups, members, per_owner)
         for load in loads[3:6]:
             load.wait()
         x = preact_ref[...].astype(F32)
@@ -82,10 +92,9 @@
             take = one_hot(dst, nodes)
             all_terms.append((dot_nn(pushed_t, take) * weight_ref[:, e0 : e0 + chunk]).astype(BF16))
         terms = jnp.concatenate(all_terms, axis=1)
-
-        sums = dot_nt(put_ref[...], terms).astype(BF16)
-        for n, (ref, j, p, _) in enumerate(pieces):
-            ref[p, j * groups : (j + 1) * groups] = sums[n * groups : (n + 1) * groups]
+        terms_ref[...] = terms
+
+        store_slots(send_ref, dot_nt(put_ref[...], terms), groups, per_owner)
 
         for load in loads[6:]:
             load.wait()
@@ -98,9 +107,19 @@
                 low = grad[2 * k * share : (2 * k + 1) * share]
                 high = grad[(2 * k + 1) * share : (2 * k + 2) * share]
                 send_ref[p, tail] = jnp.where(side == 0, high, low).astype(BF16)
-                keep_ref[p, tail] = jnp.where(side == 0, low, high).astype(BF16)
+                tail_ref[p] = jnp.where(side == 0, low, high).astype(BF16)
         for store in stores:
             store.wait()
+
+    return kernel
+
+
+def own_side(groups, members, per_owner):
+    def kernel(terms_ref, place_ref, tail_ref, keep_ref, put_ref):
+        side = lax.rem(lax.axis_index("local"), 2)
+        fill_slots(put_ref, place_ref[...], side, groups, members, per_owner)
+        store_slots(keep_ref, dot_nt(put_ref[...], terms_ref[...]), groups, per_owner)
+        keep_ref[:, per_owner * groups :] = tail_ref[...]
 
     return kernel
 
@@ -224,21 +243,23 @@
         aggregate,
     )
     half = jax.ShapeDtypeStruct((members // 2, per_owner * groups + share, width), BF16)
-    dp, pushed_t, send, keep = pl.pallas_call(
+    dp, pushed_t, send, tail, terms, place = pl.pallas_call(
         edges_and_grads(groups, members, per_owner, scale, 512),
         out_shape=(
             pltpu.HBM((nodes, width), BF16),
             pltpu.HBM((width, nodes), BF16),
             half,
-            half,
+            jax.ShapeDtypeStruct((members // 2, share, width), BF16),
+            jax.ShapeDtypeStruct((width, edges), BF16),
+            jax.ShapeDtypeStruct((1, edges), jnp.int32),
         ),
         in_specs=[hbm] * len(operands),
-        out_specs=(hbm, hbm, vmem, vmem),
+        out_specs=(hbm, hbm, vmem, vmem, vmem, vmem),
         scratch_shapes=[pltpu.VMEM(a.shape, a.dtype) for a in operands]
         + [
             pltpu.VMEM((nodes, width), BF16),
             pltpu.VMEM((width, nodes), BF16),
-            pltpu.VMEM((members * per_owner * groups, edges), BF16),
+            pltpu.VMEM((members * per_owner * groups // 2, edges), BF16),
             pltpu.SemaphoreType.DMA((len(operands),)),
             pltpu.SemaphoreType.DMA((2,)),
         ],
@@ -270,6 +291,13 @@
     other_core = [(i, i ^ 1) for i in range(members)]
     along_x = [list(range(core, members, 2)) for core in range(2)]
     came = lax.ppermute(send, "local", other_core)
+    keep = pl.pallas_call(
+        own_side(groups, members, per_owner),
+        out_shape=half,
+        scratch_shapes=[pltpu.VMEM((members * per_owner * groups // 2, edges), BF16)],
+        compiler_params=params,
+        name="own_side",
+    )(terms, place, tail)
     chip_sum = (came.astype(F32) + keep.astype(F32)).astype(BF16)
     parts = lax.all_to_all(chip_sum, "local", 0, 0, axis_index_groups=along_x, tiled=True)
     summed = pl.pallas_call(

time: 91.7 us -> 91.3 us (level)
  waiting for transfers between devices: 21.5 us -> 20.5 us
    ppermute x1, waiting for transfers between devices: 1.51 us -> 0.46 us  [on_device(): came = lax.ppermute(send, 'local', other_core)]
    pallas_call x0 -> x1, Pallas kernels: none -> 1.01 us  [on_device(): pl.pallas_call(own_side(groups, members, per_owner), out_shape=half, scra...]
  transfers between devices with their start and end apart: 3 -> 3, of which waited for: 3 -> 3; matrix products, arithmetic and copies ran while one was open for 0% -> 0% of each run, Pallas kernels for 5% -> 6%
where the time goes in v6:
time: 91.3 us; the launch traced here: 90.9 us
  starting transfers between devices  29.8 us (33%)
  blocking collectives  25.7 us (28%)
  waiting for transfers between devices  20.5 us (22%)
  Pallas kernels  12.9 us (14%)
  local copies, waits for them, and re-layouts  0.96 us (1%)
    all_to_all x1, waiting for transfers between devices, on_device(): arrived = lax.all_to_all(summed, 'group', 0, 0, tiled=True)  14.2 us
    all_to_all x1, blocking collectives, on_device(): grads = lax.all_to_all(mine, 'local', 0, 0, tiled=True)  13.9 us
    all_to_all x1, starting transfers between devices, on_device(): arrived = lax.all_to_all(summed, 'group', 0, 0, tiled=True)  13.9 us
    ppermute x1, starting transfers between devices, on_device(): came = lax.ppermute(send, 'local', other_core)  12.4 us
    all_to_all x1, blocking collectives, on_device(): lax.all_to_all(chip_sum, 'local', 0, 0, axis_index_groups=along_x, tiled=...  11.8 us
    all_to_all x1, waiting for transfers between devices, on_device(): lax.all_to_all(rows, 'group', 0, 0, axis_index_groups=blocks, tiled=True)  5.87 us
    pallas_call x1, Pallas kernels, on_device(): pl.pallas_call(edges_and_grads(groups, members, per_owner, scale, 512), o...  4.82 us
    all_to_all x1, starting transfers between devices, on_device(): lax.all_to_all(rows, 'group', 0, 0, axis_index_groups=blocks, tiled=True)  3.5 us
  transfers between devices with their start and end apart: 3, of which 3 were waited for; matrix products, arithmetic and copies ran while one was open for 0% of the time, Pallas kernels for 6%

profile of v6, /device:TPU:1, one launch (start us, length us, event | category | flops | bytes accessed | tf_op | source)
XLA Modules:
  0.0 90.9 jit_solution(9121070285076375063)
XLA Ops:
  0.6 4.8 %edges_and_grads.1 = (bf16[1024,256]{1,0:T(8,128)(2,1)}, bf16[256,1024]{1,0:T(8,128)(2,1)}, bf16[4,256,256]{2,1,0:T(8,128)(2,1)S(1)}, bf16[4,64,256]{2,1,0:T(8,1...) custom-call(s32[1,2048]{1,0:T(1,128)} %bitcast.7, s32[1,2048]{1,0:T(1,128)} %bitcast.8, ...), custom_call_target="tpu_custom_call" | custom-call | tf_op jit(solution)/shard_map/edges_and_grads/pallas_call | solution.py:246
  5.5 12.4 %collective-permute-start = (bf16[4,256,256]{2,1,0:T(8,128)(2,1)S(1)}, bf16[4,256,256]{2,1,0:T(8,128)(2,1)S(1)}, u32[]{:S(2)}, u32[]{:S(2)}) collective-permute-start(bf16[4,256,256]{2,1,0:T(8,128)(2,1)S(1)} %get-tuple-element.15), channel_id=1, source_target_pairs={{0,1},{1,0},{2,3},{3,2},{4,5},{5,4},{6,7},{7,6},{8,9},{9,8},{10,11... | collective-permute-start | bytes 1572872 | tf_op jit(solution)/shard_map/ppermute | solution.py:293
  17.9 1.0 %own_side.1 = bf16[4,256,256]{2,1,0:T(8,128)(2,1)S(1)} custom-call(bf16[256,2048]{1,0:T(8,128)(2,1)S(1)} %get-tuple-element.16.terms_ref, s32[1,2048]{1,0:T(1,128)S(1)} %get-tuple-element.17.place_ref, bf16[4,64,256]{2,1,0:T(8,128)(2,1)S(1)} %get-tuple-element.18.tail_ref), custom_call_target="tpu_custom_call" | custom-call | tf_op jit(solution)/shard_map/own_side/pallas_call | solution.py:294
  18.9 0.0 copy-start
  18.9 0.0 copy-start.3
  18.9 0.0 copy-start.4
  19.0 0.5 collective-permute-done
  19.4 0.1 add_convert_fusion
  19.6 11.8 %all_to_all.20.parts_ref = bf16[4,256,256]{2,1,0:T(8,128)(2,1)S(1)} all-to-all(bf16[4,256,256]{2,1,0:T(8,128)(2,1)S(1)} %add_convert_fusion), channel_id=1, replica_groups={{0,2,4,6},{1,3,5,7},{8,10,12,14},{9,11,13,15},{16,18,20,22},{17,19,21,2..., dimensions={0} | all-to-all | bytes 1048576 | tf_op jit(solution)/shard_map/all_to_all | solution.py:302
  31.4 1.1 %member_sum.1 = bf16[96,2,768]{2,1,0:T(2,128)(2,1)} custom-call(bf16[4,256,256]{2,1,0:T(8,128)(2,1)S(1)} %all_to_all.20.parts_ref), custom_call_target="tpu_custom_call" | custom-call | tf_op jit(solution)/shard_map/member_sum/pallas_call | solution.py:303
  32.5 13.9 %all-to-all-start.1 = ((bf16[96,2,768]{2,1,0:T(2,128)(2,1)}), bf16[96,2,768]{2,1,0:T(2,128)(2,1)S(1)}, u32[]{:S(2)}, u32[]{:S(2)}) async-start(bf16[96,2,768]{2,1,0:T(2,128)(2,1)} %member_sum.1), calls=%async_computation.1 | async-start | bytes 589824 | tf_op jit(solution)/shard_map/all_to_all | solution.py:309
  46.4 0.0 copy-done
  46.4 0.0 copy-done.3
  46.4 0.0 copy-done.4
  46.4 0.0 copy-start.1
  46.4 0.9 copy-done.1
  47.3 0.0 copy-start.2
  47.3 2.7 %tiles.1.base_ref = f32[1024,256]{1,0:T(8,128)S(1)} custom-call(s32[64]{0:T(128)S(1)} %copy-done.3, s32[64]{0:T(128)S(1)} %copy-done.4, bf16[64,128,128]{2,1,0:T(8,128)(2,1)S(1)} %copy-done, bf16[256,1024]{1,0:T(8,128)(2,1)} %get-tuple-element.19.pushed_hbm, bf16[1024,256]{1,0:T(8,128)(2,1)} %get-tuple-element.20.dp_hbm, bf16[256,256]{1,0:T(8,128)(2,1)S(1)} %copy-done.1), custom_call_target="tpu_custom_call" | custom-call | tf_op jit(solution)/shard_map/tiles/pallas_call | solution.py:269
  50.0 14.2 %all-to-all-done.1.arrived_ref = bf16[96,2,768]{2,1,0:T(2,128)(2,1)S(1)} async-done(((bf16[96,2,768]{2,1,0:T(2,128)(2,1)}), bf16[96,2,768]{2,1,0:T(2,128)(2,1)S(1)}, u32[]{:S(2)}, u32[]{:S(2)}) %all-to-all-start.1) | async-done | bytes 294944 | tf_op jit(solution)/shard_map/all_to_all | solution.py:309
  64.3 0.9 grad_rows.1
  65.1 3.5 %all-to-all-start.2 = ((bf16[16,8,128]{2,1,0:T(8,128)(2,1)}), bf16[16,8,128]{2,1,0:T(8,128)(2,1)S(1)}, u32[]{:S(2)}, u32[]{:S(2)}) async-start(bf16[16,8,128]{2,1,0:T(8,128)(2,1)} %grad_rows.1), calls=%async_computation.2 | async-start | bytes 65536 | tf_op jit(solution)/shard_map/all_to_all | solution.py:318
  68.6 0.0 copy-done.2
  68.6 1.4 %finish.1 = bf16[1024,256]{1,0:T(8,128)(2,1)} custom-call(bf16[96,2,768]{2,1,0:T(2,128)(2,1)S(1)} %all-to-all-done.1.arrived_ref, s32[2,96]{1,0:T(2,128)S(1)} %bitcast.6, f32[1024,256]{1,0:T(8,128)S(1)} %tiles.1.base_ref), custom_call_target="tpu_custom_call" | custom-call | tf_op jit(solution)/shard_map/finish/pallas_call | solution.py:319
  70.1 5.9 %all-to-all-done.2 = bf16[16,8,128]{2,1,0:T(8,128)(2,1)S(1)} async-done(((bf16[16,8,128]{2,1,0:T(8,128)(2,1)}), bf16[16,8,128]{2,1,0:T(8,128)(2,1)S(1)}, u32[]{:S(2)}, u32[]{:S(2)}) %all-to-all-start.2) | async-done | bytes 32800 | tf_op jit(solution)/shard_map/all_to_all | solution.py:318
  76.0 13.9 %all_to_all.21.grads_ref = bf16[8,16,8,128]{3,2,1,0:T(8,128)(2,1)S(1)} all-to-all(bf16[8,16,8,128]{3,2,1,0:T(8,128)(2,1)S(1)} %broadcast_in_dim.2), channel_id=1, replica_groups=mesh['group'=96,'local'=8] {'local'}, dimensions={0} | all-to-all | bytes 524288 | tf_op jit(solution)/shard_map/all_to_all | solution.py:327
  89.9 1.0 %widen.1 = (f32[256,256]{1,0:T(8,128)}, f32[256,256]{1,0:T(8,128)}) custom-call(bf16[8,16,8,128]{3,2,1,0:T(8,128)(2,1)S(1)} %all_to_all.21.grads_ref), custom_call_target="tpu_custom_call" | custom-call | tf_op jit(solution)/shard_map/widen/pallas_call | solution.py:328
  (1 shorter events, 0.0 us)
Async XLA Ops:
  5.5 14.0 %collective-permute-start = (bf16[4,256,256]{2,1,0:T(8,128)(2,1)S(1)}, bf16[4,256,256]{2,1,0:T(8,128)(2,1)S(1)}, u32[]{:S(2)}, u32[]{:S(2)}) collective-permute-start(bf16[4,256,256]{2,1,0:T(8,128)(2,1)S(1)} %get-tuple-element.15), channel_id=1, source_target_pairs={{0,1},{1,0},{2,3},{3,2},{4,5},{5,4},{6,7},{7,6},{8,9},{9,8},{10,11... | collective-permute-start | bytes 1572872 | tf_op jit(solution)/shard_map/ppermute | solution.py:293
  18.9 27.4 %copy-start = (bf16[64,128,128]{2,1,0:T(8,128)(2,1)S(1)}, bf16[64,128,128]{2,1,0:T(8,128)(2,1)}, u32[]{:S(2)}) copy-start(bf16[64,128,128]{2,1,0:T(8,128)(2,1)} %vals_ref.1) | copy-start | bytes 6291460
  18.9 27.4 %copy-start.3 = (s32[64]{0:T(128)S(1)}, s32[64]{0:T(128)}, u32[]{:S(2)}) copy-start(s32[64]{0:T(128)} %rows_ref.1) | copy-start | bytes 772
  18.9 27.4 %copy-start.4 = (s32[64]{0:T(128)S(1)}, s32[64]{0:T(128)}, u32[]{:S(2)}) copy-start(s32[64]{0:T(128)} %cols_ref.1) | copy-start | bytes 772
  32.5 31.8 %all-to-all-start.1 = ((bf16[96,2,768]{2,1,0:T(2,128)(2,1)}), bf16[96,2,768]{2,1,0:T(2,128)(2,1)S(1)}, u32[]{:S(2)}, u32[]{:S(2)}) async-start(bf16[96,2,768]{2,1,0:T(2,128)(2,1)} %member_sum.1), calls=%async_computation.1 | async-start | bytes 589824 | tf_op jit(solution)/shard_map/all_to_all | solution.py:309
  46.4 0.9 copy-start.1
  47.3 21.3 %copy-start.2 = (s32[1,96,2]{1,2,0:T(2,128)S(1)}, s32[1,96,2]{1,2,0:T(2,128)}, u32[]{:S(2)}) copy-start(s32[1,96,2]{1,2,0:T(2,128)} %param.25) | copy-start | bytes 2308
  65.1 10.8 %all-to-all-start.2 = ((bf16[16,8,128]{2,1,0:T(8,128)(2,1)}), bf16[16,8,128]{2,1,0:T(8,128)(2,1)S(1)}, u32[]{:S(2)}, u32[]{:S(2)}) async-start(bf16[16,8,128]{2,1,0:T(8,128)(2,1)} %grad_rows.1), calls=%async_computation.2 | async-start | bytes 65536 | tf_op jit(solution)/shard_map/all_to_all | solution.py:318
